TPU v7x, 32 devices: a whole 2x2x4 slice. The times are simulated.
32 devices in a mesh: rows: 4 (over z), feat: 8 (over y, x, core).
Axes of the slice: x: 2, y: 2, z: 4, core: 2. Of those that a mesh axis runs over, the one named last changes fastest.
Arguments:
- bins: int32 [65536, 256], P(('rows', 'feat')), may hold values from 0 to 15
- node_of: int32 [65536], P(('rows', 'feat')), may hold values from 0 to 64
- weight: float32 [65536], P(('rows', 'feat')), may hold values from 0.25 to 4
- label: float32 [65536], P(('rows', 'feat')), may hold values from -6 to 6
- split_bins: int32 [64, 256], P('rows', 'feat'), may hold values from 0 to 14
Outputs:
- gain: float32 [64, 256], P('rows', 'feat')
- node_best: float32 [64], P('rows')
All inputs are finite; a program needn't handle non-finite values.
Results may differ from a plain program's by a relative error of at most 0.0035.
Values sent between devices are 32-bit elements; how exact they have to be, the bound alone decides.
No kernel may reach another device: no remote copies, remote signals or barrier semaphores. Data moves between devices by JAX's collectives and lax.ppermute only.
A program may use at most 64 MiB of HBM per device.

v0:
```python
import jax
import jax.numpy as jnp
from jax import lax
from jax.sharding import PartitionSpec as P

B = 16


def shards(bins, node_of, weight, label, split_bins):
    rows_here = bins.shape[0]
    feats = bins.shape[1]
    nodes = split_bins.shape[0] * lax.axis_size("rows")
    block = min(512, rows_here)
    w16 = weight.astype(jnp.bfloat16)
    wy16 = (weight * label).astype(jnp.bfloat16)
    bin_ids = jnp.arange(B, dtype=jnp.int32)
    node_ids = jnp.arange(nodes, dtype=jnp.int32)

    def add_block(step, accum):
        start = step * block
        bin_blk = lax.dynamic_slice_in_dim(bins, start, block, 0)
        node_blk = lax.dynamic_slice_in_dim(node_of, start, block, 0)
        w_blk = lax.dynamic_slice_in_dim(w16, start, block, 0)
        wy_blk = lax.dynamic_slice_in_dim(wy16, start, block, 0)
        onehot = (
            (bin_blk[:, :, None] == bin_ids[None, None, :])
            .astype(jnp.bfloat16)
            .reshape(block, feats * B)
        )
        node_hot = (node_blk[:, None] == node_ids[None, :]).astype(jnp.bfloat16)
        left_side = jnp.concatenate([node_hot * w_blk[:, None], node_hot * wy_blk[:, None]], axis=1)
        return accum + lax.dot_general(
            left_side, onehot, (((0,), (0,)), ((), ())), preferred_element_type=jnp.float32
        )

    partial_hist = lax.fori_loop(
        0, rows_here // block, add_block, jnp.zeros((2 * nodes, feats * B), jnp.float32)
    )
    n_rows = lax.axis_size("rows")
    n_feat = lax.axis_size("feat")
    node_part = nodes // n_rows
    feat_width = feats * B // n_feat
    arranged = partial_hist.reshape(2, n_rows, node_part, n_feat, feat_width).transpose(
        1, 3, 0, 2, 4
    )
    arranged = arranged.reshape(n_rows * n_feat, 2, node_part, feat_width)
    owned = lax.psum_scatter(arranged, ("rows", "feat"), scatter_dimension=0, tiled=True)
    hist = owned.reshape(2, node_part, feat_width // B, B)
    total = jnp.sum(hist, axis=-1)
    mask = (bin_ids[None, None, :] <= split_bins[:, :, None]).astype(jnp.float32)
    left = jnp.sum(hist * mask[None], axis=-1)
    right = total - left
    gain = (
        left[1] ** 2 / (left[0] + 1.0)
        + right[1] ** 2 / (right[0] + 1.0)
        - total[1] ** 2 / (total[0] + 1.0)
    ) / (total[0] + 1.0)
    node_best = lax.pmax(jnp.max(gain, axis=1), "feat")
    return (gain, node_best)


def solution(mesh):
    placed = (
        P(("rows", "feat"), None),
        P(("rows", "feat")),
        P(("rows", "feat")),
        P(("rows", "feat")),
        P("rows", "feat"),
    )
    return jax.shard_map(
        shards,
        mesh=mesh,
        in_specs=placed,
        out_specs=(P("rows", "feat"), P("rows")),
        check_vma=False,
    )
```

profile of v0, /device:TPU:0, one launch (start us, length us, event | category | flops | bytes accessed | tf_op | source)
XLA Modules:
  0.0 207.5 jit_solution(6475228254082957907)
XLA Ops:
  7.2 0.8 multiply_convert_fusion
  8.0 33.3 %while.14 = (s32[]{:T(128)}, f32[128,4096]{1,0:T(8,128)}, s32[2048]{0:T(1024)}, bf16[2048]{0:T(1024)(128)(2,1)S(1)}, bf16[2048]{0:T(1024)(128)(2,1)S(1)}, /*inde...) while((s32[]{:T(128)}, f32[128,4096]{1,0:T(8,128)}, s32[2048]{0:T(1024)}, ...), condition=%wide.region_1.0_spmd.clone, body=%wide.region_0.0_spmd.clone.sunk | while | flops 540377088 | bytes 11350189 | solution.py:36
  8.0 0.8 dynamic_slice.38
  9.2 1.1 constant_dynamic-slice_fusion.2
  10.6 1.5 bitcast_compare_fusion.2
  12.1 3.0 %convolution_add_fusion.2 = f32[128,4096]{1,0:T(8,128)} fusion(pred[512,4096]{0,1:T(32,128)(4,1)S(1)} %bitcast_compare_fusion.2, f32[128,4096]{1,0:T(8,128)} %get-tuple-element.251, pred[]{:T(512)S(6)} %compare.3, bf16[512,64]{1,0:T(8,128)(2,1)S(1)} %get-tuple-element.238, bf16[512,64]{1,0:T(8,128)(2,1)S(1)} %get-tuple-element.239), kind=kOutput, calls=%fused_computation.3.clone.1 | convolution fusion | flops 538181632 | bytes 6422529 | tf_op jit(solution)/shard_map/while/body/eval_jaxpr/dot_general | solution.py:32
  15.1 0.8 dynamic_slice.38
  16.3 1.1 constant_dynamic-slice_fusion.2
  17.7 1.5 bitcast_compare_fusion.2
  19.2 4.6 %convolution_add_fusion.2 = f32[128,4096]{1,0:T(8,128)} fusion(pred[512,4096]{0,1:T(32,128)(4,1)S(1)} %bitcast_compare_fusion.2, f32[128,4096]{1,0:T(8,128)} %get-tuple-element.251, pred[]{:T(512)S(6)} %compare.3, bf16[512,64]{1,0:T(8,128)(2,1)S(1)} %get-tuple-element.238, bf16[512,64]{1,0:T(8,128)(2,1)S(1)} %get-tuple-element.239), kind=kOutput, calls=%fused_computation.3.clone.1 | convolution fusion | flops 538181632 | bytes 6422529 | tf_op jit(solution)/shard_map/while/body/eval_jaxpr/dot_general | solution.py:32
  23.8 0.8 dynamic_slice.38
  25.0 1.1 constant_dynamic-slice_fusion.2
  26.4 1.5 bitcast_compare_fusion.2
  28.0 4.6 %convolution_add_fusion.2 = f32[128,4096]{1,0:T(8,128)} fusion(pred[512,4096]{0,1:T(32,128)(4,1)S(1)} %bitcast_compare_fusion.2, f32[128,4096]{1,0:T(8,128)} %get-tuple-element.251, pred[]{:T(512)S(6)} %compare.3, bf16[512,64]{1,0:T(8,128)(2,1)S(1)} %get-tuple-element.238, bf16[512,64]{1,0:T(8,128)(2,1)S(1)} %get-tuple-element.239), kind=kOutput, calls=%fused_computation.3.clone.1 | convolution fusion | flops 538181632 | bytes 6422529 | tf_op jit(solution)/shard_map/while/body/eval_jaxpr/dot_general | solution.py:32
  32.6 0.8 dynamic_slice.38
  33.8 1.1 constant_dynamic-slice_fusion.2
  35.2 1.5 bitcast_compare_fusion.2
  36.7 4.6 %convolution_add_fusion.2 = f32[128,4096]{1,0:T(8,128)} fusion(pred[512,4096]{0,1:T(32,128)(4,1)S(1)} %bitcast_compare_fusion.2, f32[128,4096]{1,0:T(8,128)} %get-tuple-element.251, pred[]{:T(512)S(6)} %compare.3, bf16[512,64]{1,0:T(8,128)(2,1)S(1)} %get-tuple-element.238, bf16[512,64]{1,0:T(8,128)(2,1)S(1)} %get-tuple-element.239), kind=kOutput, calls=%fused_computation.3.clone.1 | convolution fusion | flops 538181632 | bytes 6422529 | tf_op jit(solution)/shard_map/while/body/eval_jaxpr/dot_general | solution.py:32
  41.3 3.2 %copy.11 = f32[16,8,8,512]{3,2,1,0:T(8,128)S(1)} copy(f32[16,8,8,512]{3,1,2,0:T(8,128)} %bitcast.34) | data formatting | bytes 4194304
  44.5 2.6 %copy.9 = f32[4,8,2,16,512]{4,3,2,1,0:T(8,128)} copy(f32[4,8,2,16,512]{4,1,3,0,2:T(8,128)S(1)} %bitcast.36) | data formatting | bytes 4194304 | tf_op jit(solution)/shard_map/transpose | solution.py:43
  47.9 138.3 %reduce-scatter.2.cloned.1.call-done = f32[1,2,16,512]{3,2,1,0:T(8,128)} async-done(((f32[32,2,16,512]{3,2,1,0:T(8,128)}), f32[1,2,16,512]{3,2,1,0:T(8,128)}) %reduce-scatter.2.cloned.1.call-update) | async-done | bytes 65552 | tf_op jit(solution)/shard_map/reduce_scatter | solution.py:47
  186.2 1.0 reshape.51
  187.6 0.7 fusion.20
  188.3 12.3 %pmax.7 = f32[16]{0:T(128)} all-reduce(f32[16]{0:T(128)S(1)} %get-tuple-element.193), channel_id=1, replica_groups=mesh['rows'=4,'feat'=8] {'feat'}, use_global_device_ids=true, to_apply=%region_6.0 | all-reduce | flops 16 | bytes 128 | tf_op jit(solution)/shard_map/pmax | solution.py:58
  (32 shorter events, 4.1 us)
Async XLA Ops:
  7.2 179.0 %reduce-scatter.2.cloned.1.call-start = ((), (), s32[]{:S(2)}) async-start(), calls=%async_computation.1 | async-start | bytes 2162688 | tf_op jit(solution)/shard_map/reduce_scatter | solution.py:47
  47.1 0.7 copy-start
Sparse Core Ops, SparseCore 0:
  47.2 138.9 reduce-scatter.1
where the time goes:
time: 208 us; the launch traced here: 207 us
  waiting for transfers between devices  138 us (66%)
  matrix products  16.9 us (8%)
  local copies, waits for them, and re-layouts  16.7 us (8%)
  between operations  14.1 us (7%)
  blocking collectives  12.3 us (6%)
  other arithmetic  9.04 us (4%)
    reduce_scatter x1, waiting for transfers between devices, shards(): lax.psum_scatter(arranged, ('rows', 'feat'), scatter_dimension=0, tiled=T...  138 us
    dot_general x4, matrix products, add_block(): lax.dot_general(left_side, onehot, (((0,), (0,)), ((), ())), preferred_el...  16.9 us
    pmax x1, blocking collectives, shards(): node_best = lax.pmax(jnp.max(gain, axis=1), 'feat')  12.3 us
    eq x4, other arithmetic, add_block(): bin_blk[:, :, None] == bin_ids[None, None, :]  5.99 us
    dynamic_slice x8, local copies, waits for them, and re-layouts, add_block(): bin_blk = lax.dynamic_slice_in_dim(bins, start, block, 0)  5.12 us
  transfers between devices with their start and end apart: 1, of which 1 were waited for; matrix products, arithmetic and copies ran while one was open for 0% of the time, Pallas kernels for 0%

commit v1 on v0

v1 whole, which is shorter than its diff:
```python
import jax
import jax.numpy as jnp
from jax import lax
from jax.sharding import Mesh, PartitionSpec as P

ALL = ("rows", "chip", "core")


def shards(bins, node_of, weight, label, split_bins):
    n_rows = lax.axis_size("rows")
    n_chip = lax.axis_size("chip")
    n_all = n_rows * n_chip * 2
    core = lax.axis_index("core")
    rows_here, feats = bins.shape
    node_part, feat_part = split_bins.shape
    nodes = node_part * n_rows
    half_f = feats // 2
    half_n = node_part // 2
    w16 = weight.astype(jnp.bfloat16)
    wy16 = (weight * label).astype(jnp.bfloat16)
    node_hot = jnp.arange(nodes, dtype=jnp.int32)[:, None] == node_of[None, :]
    zero = jnp.bfloat16(0)
    sides = jnp.concatenate(
        [jnp.where(node_hot, w16[None], zero), jnp.where(node_hot, wy16[None], zero)], axis=0
    )
    total_here = jnp.sum(sides.astype(jnp.float32), axis=1)

    block = jnp.concatenate([split_bins.reshape(-1).astype(jnp.float32), total_here])
    got = lax.all_to_all(
        jnp.broadcast_to(block[None], (n_all, block.shape[0])), ALL, 0, 0, tiled=True
    )
    total = jnp.sum(got[:, node_part * feat_part :], axis=0).reshape(2, nodes)
    splits = (
        got[:, : node_part * feat_part]
        .reshape(n_rows, n_chip * 2, node_part, feat_part)
        .transpose(0, 2, 1, 3)
        .reshape(nodes, feats)
        .astype(jnp.bfloat16)
    )

    row_split = lax.dot_general(
        node_hot.astype(jnp.bfloat16), splits, (((0,), (0,)), ((), ())),
        preferred_element_type=jnp.float32,
    )
    mask = (bins.astype(jnp.float32) <= row_split).astype(jnp.bfloat16)
    left = jnp.dot(sides, mask, preferred_element_type=jnp.float32)

    pair = [(0, 1), (1, 0)]
    mine = lax.dynamic_slice_in_dim(left, core * half_f, half_f, 1)
    other = lax.dynamic_slice_in_dim(left, (1 - core) * half_f, half_f, 1)
    mine = mine + lax.ppermute(other, "core", pair)

    parts = mine.reshape(2, n_rows, 2, half_n, half_f).transpose(1, 2, 0, 3, 4)
    parts = jnp.broadcast_to(
        parts[:, None], (n_rows, n_chip, 2, 2, half_n, half_f)
    ).reshape(n_all, 2, half_n, half_f)
    parts = lax.all_to_all(parts, ALL, 0, 0, tiled=True)
    left = jnp.sum(parts.reshape(n_rows * n_chip, 2, 2, half_n, half_f), axis=0)
    left = left.transpose(1, 2, 0, 3).reshape(2, half_n, feats)

    first = lax.axis_index("rows") * node_part + core * half_n
    total = lax.dynamic_slice_in_dim(total, first, half_n, 1)[:, :, None]
    right = total - left
    gain = (
        left[1] ** 2 / (left[0] + 1.0)
        + right[1] ** 2 / (right[0] + 1.0)
        - total[1] ** 2 / (total[0] + 1.0)
    ) / (total[0] + 1.0)
    theirs = lax.ppermute(gain, "core", pair)
    gain = jnp.where(
        core == 0, jnp.concatenate([gain, theirs]), jnp.concatenate([theirs, gain])
    )
    own = (lax.axis_index("chip") * 2 + core) * feat_part
    return lax.dynamic_slice_in_dim(gain, own, feat_part, 1), jnp.max(gain, axis=1)


def solution(mesh):
    n_rows, n_feat = mesh.devices.shape
    cores = Mesh(mesh.devices.reshape(n_rows, n_feat // 2, 2), ALL)
    placed = (P(ALL, None), P(ALL), P(ALL), P(ALL), P("rows", ("chip", "core")))
    return jax.shard_map(
        shards,
        mesh=cores,
        in_specs=placed,
        out_specs=(P("rows", ("chip", "core")), P("rows")),
        check_vma=False,
    )
```

time: 208 us -> 38.5 us (0.19)
  waiting for transfers between devices: 138 us -> 20.3 us
  matrix products: 16.9 us -> 0.86 us
  local copies, waits for them, and re-layouts: 16.7 us -> 2.64 us
  between operations: 14.1 us -> 0.77 us
  blocking collectives: 12.3 us -> 0 us
  starting transfers between devices: 0.04 us -> 10.1 us
  other arithmetic: 9.04 us -> 3.4 us
    reduce_scatter x1 -> x0, waiting for transfers between devices: 138 us -> none  [shards(): lax.psum_scatter(arranged, ('rows', 'feat'), scatter_dimension=0, tiled=T...]
    all_to_all x0 -> x2, waiting for transfers between devices: none -> 18.1 us  [the longest x1 10.5 us: shards(): parts = lax.all_to_all(parts, ALL, 0, 0, tiled=True)]
    dot_general x4 -> x1, matrix products: 16.9 us -> 0.86 us  [shards(): left = jnp.dot(sides, mask, preferred_element_type=jnp.float32)]
    pmax x1 -> x0, blocking collectives: 12.3 us -> none  [shards(): node_best = lax.pmax(jnp.max(gain, axis=1), 'feat')]
    all_to_all x0 -> x2, starting transfers between devices: none -> 9.88 us  [the longest x1 7.3 us: shards(): lax.all_to_all(jnp.broadcast_to(block[None], (n_all, block.shape[0])), AL...]
    dynamic_slice x20 -> x3, local copies, waits for them, and re-layouts: 8.76 us -> 0.76 us  [the longest x1 0.67 us: shards(): lax.dynamic_slice_in_dim(gain, own, feat_part, 1)]
    eq x4 -> x0, other arithmetic: 5.99 us -> none  [add_block(): bin_blk[:, :, None] == bin_ids[None, None, :]]
    unnamed x3 -> x5, local copies, waits for them, and re-layouts: 3.9 us -> 0.02 us
  transfers between devices with their start and end apart: 1 -> 4, of which waited for: 1 -> 4; matrix products, arithmetic and copies ran while one was open for 0% -> 1% of each run, Pallas kernels for 0% -> 0%
where the time goes in v1:
time: 38.5 us; the launch traced here: 38 us
  waiting for transfers between devices  20.3 us (53%)
  starting transfers between devices  10.1 us (26%)
  other arithmetic  3.4 us (9%)
  local copies, waits for them, and re-layouts  2.64 us (7%)
  matrix products  0.86 us (2%)
  between operations  0.77 us (2%)
    all_to_all x1, waiting for transfers between devices, shards(): parts = lax.all_to_all(parts, ALL, 0, 0, tiled=True)  10.5 us
    all_to_all x1, waiting for transfers between devices, shards(): lax.all_to_all(jnp.broadcast_to(block[None], (n_all, block.shape[0])), AL...  7.59 us
    all_to_all x1, starting transfers between devices, shards(): lax.all_to_all(jnp.broadcast_to(block[None], (n_all, block.shape[0])), AL...  7.3 us
    all_to_all x1, starting transfers between devices, shards(): parts = lax.all_to_all(parts, ALL, 0, 0, tiled=True)  2.58 us
    ppermute x1, waiting for transfers between devices, shards(): theirs = lax.ppermute(gain, 'core', pair)  1.15 us
    ppermute x1, waiting for transfers between devices, shards(): mine = mine + lax.ppermute(other, 'core', pair)  1.03 us
    dot_general x1, matrix products, shards(): left = jnp.dot(sides, mask, preferred_element_type=jnp.float32)  0.86 us
    convert_element_type x1, other arithmetic, shards(): split_bins.reshape(-1).astype(jnp.float32)  0.85 us
  transfers between devices with their start and end apart: 4, of which 4 were waited for; matrix products, arithmetic and copies ran while one was open for 1% of the time, Pallas kernels for 0%

profile of v1, /device:TPU:0, one launch (start us, length us, event | category | flops | bytes accessed | tf_op | source)
XLA Modules:
  0.0 38.0 jit_solution(11451796250718334370)
XLA Ops:
  0.7 0.8 %convert_element_type.33 = f32[16,32]{1,0:T(8,128)S(1)} convert(s32[16,32]{1,0:T(8,128)} %param.9) | non-fusion elementwise | flops 512 | bytes 4096 | tf_op jit(solution)/shard_map/convert_element_type | solution.py:28
  1.5 0.1 convert_element_type.34
  1.6 0.8 %fusion.14 = (bf16[2048]{0:T(1024)(128)(2,1)S(1)}, bf16[2048]{0:T(1024)(128)(2,1)S(1)}) fusion(f32[2048]{0:T(1024)} %param.7, f32[2048]{0:T(1024)} %param.8), kind=kLoop, calls=%fused_computation.34 | loop fusion | flops 6144 | bytes 24576 | tf_op jit(solution)/shard_map/convert_element_type | solution.py:19
  2.4 0.8 %fusion.2 = (bf16[64,2048]{1,0:T(8,128)(2,1)S(1)}, bf16[64,2048]{1,0:T(8,128)(2,1)S(1)}) fusion(s32[2048]{0:T(1024)} %param.6, bf16[2048]{0:T(1024)(128)(2,1)S(1)} %get-tuple-element.6, bf16[2048]{0:T(1024)(128)(2,1)S(1)} %get-tuple-element.7), kind=kLoop, calls=%fused_computation.6 | loop fusion | flops 393216 | bytes 540672 | tf_op jit(solution)/shard_map/jit(_where)/select_n | solution.py:24
  3.1 0.2 convert_reduce_fusion
  3.3 0.7 %broadcast_in_dim.38 = f32[32,1,640]{2,1,0:T(1,128)} broadcast(f32[640]{0:T(1024)S(1)} %pad_maximum_fusion.2), dimensions={2} | broadcast | bytes 84480 | tf_op jit(solution)/shard_map/broadcast_in_dim | solution.py:30
  4.0 7.3 %all-to-all-start = ((f32[32,1,640]{2,1,0:T(1,128)}), f32[32,1,640]{2,1,0:T(1,128)S(1)}, u32[]{:S(2)}, u32[]{:S(2)}) async-start(f32[32,1,640]{2,1,0:T(1,128)} %broadcast_in_dim.38), calls=%async_computation | async-start | bytes 163840 | tf_op jit(solution)/shard_map/all_to_all | solution.py:29
  11.3 7.6 %all-to-all-done = f32[32,1,640]{2,1,0:T(1,128)S(1)} async-done(((f32[32,1,640]{2,1,0:T(1,128)}), f32[32,1,640]{2,1,0:T(1,128)S(1)}, u32[]{:S(2)}, u32[]{:S(2)}) %all-to-all-start) | async-done | bytes 81952 | tf_op jit(solution)/shard_map/all_to_all | solution.py:29
  18.9 0.1 convert_element_type.36
  19.1 0.1 convert_element_type.38
  19.2 0.9 %fusion = f32[128,256]{1,0:T(8,128)S(1)} fusion(bf16[64,256]{1,0:T(8,128)(2,1)S(1)} %convert_element_type.38, s32[2048,256]{1,0:T(8,128)S(1)} %copy-done, bf16[64,2048]{1,0:T(8,128)(2,1)S(1)} %get-tuple-element.5, bf16[64,2048]{1,0:T(8,128)(2,1)S(1)} %get-tuple-element.4, s32[2048]{0:T(1024)S(1)} %copy-done.1), kind=kOutput, calls=%fused_computation.1 | convolution fusion | flops 203554816 | bytes 2793472 | tf_op jit(solution)/shard_map/dot_general | solution.py:46
  20.1 0.2 collective-permute-start
  20.3 0.1 reshape.77
  20.4 1.0 %collective-permute-done = f32[128,128]{1,0:T(8,128)S(1)} collective-permute-done((f32[128,128]{1,0:T(8,128)S(1)}, f32[128,128]{1,0:T(8,128)S(1)}, u32[]{:S(2)}, u32[]{:S(2)}) %collective-permute-start) | collective-permute-done | bytes 65568 | tf_op jit(solution)/shard_map/ppermute | solution.py:51
  21.5 0.7 %broadcast_in_dim.39 = f32[4,4,2,2,8,128]{5,4,3,2,1,0:T(8,128)} broadcast(f32[4,2,2,8,128]{4,3,2,1,0:T(8,128)S(1)} %copy.16), dimensions={0,2,3,4,5} | broadcast | bytes 327680 | tf_op jit(solution)/shard_map/broadcast_in_dim | solution.py:54
  22.2 2.6 %all-to-all-start.1 = ((f32[32,2,8,128]{3,2,1,0:T(8,128)}), f32[32,2,8,128]{3,2,1,0:T(8,128)S(1)}, u32[]{:S(2)}, u32[]{:S(2)}) async-start(f32[32,2,8,128]{3,2,1,0:T(8,128)} %bitcast.3), calls=%async_computation.1 | async-start | bytes 524288 | tf_op jit(solution)/shard_map/all_to_all | solution.py:57
  24.8 0.1 constant_dynamic-slice_fusion.1
  24.9 10.5 %all-to-all-done.1 = f32[32,2,8,128]{3,2,1,0:T(8,128)S(1)} async-done(((f32[32,2,8,128]{3,2,1,0:T(8,128)}), f32[32,2,8,128]{3,2,1,0:T(8,128)S(1)}, u32[]{:S(2)}, u32[]{:S(2)}) %all-to-all-start.1) | async-done | bytes 262176 | tf_op jit(solution)/shard_map/all_to_all | solution.py:57
  35.4 0.1 bitcast_subtract_fusion
  35.5 0.1 fusion.9
  35.6 0.0 collective-permute-start.1
  35.6 1.1 %collective-permute-done.1 = f32[8,256]{1,0:T(8,128)S(1)} collective-permute-done((f32[8,256]{1,0:T(8,128)S(1)}, f32[8,256]{1,0:T(8,128)S(1)}, u32[]{:S(2)}, u32[]{:S(2)}) %collective-permute-start.1) | collective-permute-done | bytes 8224 | tf_op jit(solution)/shard_map/ppermute | solution.py:69
  36.7 0.6 %fusion.13 = (f32[16]{0:T(128)}, f32[16,256]{1,0:T(8,128)S(1)}) fusion(f32[8,256]{1,0:T(8,128)S(1)} %fusion.9, f32[8,256]{1,0:T(8,128)S(1)} %collective-permute-done.1, pred[]{:T(512)S(6)} %eq.16), kind=kLoop, calls=%fused_computation.33 | loop fusion | flops 16368 | bytes 32833 | tf_op jit(solution)/shard_map/reduce_max | solution.py:74
  37.4 0.7 %constant_dynamic-slice_fusion = f32[16,32]{1,0:T(8,128)} fusion(f32[16,256]{1,0:T(8,128)S(1)} %get-tuple-element.3, s32[]{:T(128)S(6)} %select_n.34), kind=kLoop, calls=%fused_computation.27 | loop fusion | bytes 4100 | tf_op jit(solution)/shard_map/dynamic_slice | solution.py:74
  (15 shorter events, 0.2 us)
Async XLA Ops:
  0.6 18.6 %copy-start.1 = (s32[2048]{0:T(1024)S(1)}, s32[2048]{0:T(1024)}, u32[]{:S(2)}) copy-start(s32[2048]{0:T(1024)} %param.6) | copy-start | bytes 24580
  0.6 18.6 %copy-start = (s32[2048,256]{1,0:T(8,128)S(1)}, s32[2048,256]{1,0:T(8,128)}, u32[]{:S(2)}) copy-start(s32[2048,256]{1,0:T(8,128)} %param.5) | copy-start | bytes 6291460
  4.0 14.9 %all-to-all-start = ((f32[32,1,640]{2,1,0:T(1,128)}), f32[32,1,640]{2,1,0:T(1,128)S(1)}, u32[]{:S(2)}, u32[]{:S(2)}) async-start(f32[32,1,640]{2,1,0:T(1,128)} %broadcast_in_dim.38), calls=%async_computation | async-start | bytes 163840 | tf_op jit(solution)/shard_map/all_to_all | solution.py:29
  20.1 1.3 %collective-permute-start = (f32[128,128]{1,0:T(8,128)S(1)}, f32[128,128]{1,0:T(8,128)S(1)}, u32[]{:S(2)}, u32[]{:S(2)}) collective-permute-start(f32[128,128]{1,0:T(8,128)S(1)} %constant_dynamic-slice_fusion.2), channel_id=1, source_target_pairs={{0,1},{1,0},{2,3},{3,2},{4,5},{5,4},{6,7},{7,6},{8,9},{9,8},{10,11... | collective-permute-start | bytes 196616 | tf_op jit(solution)/shard_map/ppermute | solution.py:51
  22.2 13.2 %all-to-all-start.1 = ((f32[32,2,8,128]{3,2,1,0:T(8,128)}), f32[32,2,8,128]{3,2,1,0:T(8,128)S(1)}, u32[]{:S(2)}, u32[]{:S(2)}) async-start(f32[32,2,8,128]{3,2,1,0:T(8,128)} %bitcast.3), calls=%async_computation.1 | async-start | bytes 524288 | tf_op jit(solution)/shard_map/all_to_all | solution.py:57
  35.6 1.2 %collective-permute-start.1 = (f32[8,256]{1,0:T(8,128)S(1)}, f32[8,256]{1,0:T(8,128)S(1)}, u32[]{:S(2)}, u32[]{:S(2)}) collective-permute-start(f32[8,256]{1,0:T(8,128)S(1)} %fusion.9), channel_id=1, source_target_pairs={{0,1},{1,0},{2,3},{3,2},{4,5},{5,4},{6,7},{7,6},{8,9},{9,8},{10,11... | collective-permute-start | bytes 24584 | tf_op jit(solution)/shard_map/ppermute | solution.py:69

commit v2 on v1

v2 whole, which is shorter than its diff:
```python
import jax
import jax.numpy as jnp
from jax import lax
from jax.experimental import pallas as pl
from jax.experimental.pallas import tpu as pltpu
from jax.sharding import Mesh, PartitionSpec as P

ALL = ("rows", "chip", "core")
LANES = 128
TILE = 8
PARTS = 4
VMEM = pl.BlockSpec(memory_space=pltpu.VMEM)
HBM = pl.BlockSpec(memory_space=pltpu.HBM)


def call(kernel, outs, *args, place=VMEM, scratch=()):
    if place is HBM:
        args = [pltpu.with_memory_space_constraint(x, pltpu.HBM) for x in args]
    size = sum(x.size * x.dtype.itemsize for x in (*args, *outs))
    return pl.pallas_call(
        kernel,
        out_shape=outs,
        in_specs=[place] * len(args),
        out_specs=tuple([VMEM] * len(outs)),
        scratch_shapes=list(scratch),
        compiler_params=pltpu.CompilerParams(vmem_limit_bytes=16 << 20),
        cost_estimate=pl.CostEstimate(flops=0, bytes_accessed=size, transcendentals=0),
    )(*args)


def f32(*shape):
    return jax.ShapeDtypeStruct(shape, jnp.float32)


def bf16(*shape):
    return jax.ShapeDtypeStruct(shape, jnp.bfloat16)


def announce(nodes, groups, lines, bins_hbm, node_hbm, weight_hbm, label_hbm, split_hbm,
             out_ref, sides_ref, hot_ref, bins_ref, node_ref, weight_ref, label_ref, split_ref, sems):
    copies = [
        pltpu.make_async_copy(src, dst, sems.at[k])
        for k, (src, dst) in enumerate(
            ((node_hbm, node_ref), (weight_hbm, weight_ref), (label_hbm, label_ref),
             (split_hbm, split_ref))
        )
    ]
    for c in copies:
        c.start()
    part = bins_ref.shape[0] // PARTS
    slabs = [
        pltpu.make_async_copy(
            bins_hbm.at[pl.ds(k * part, part)], bins_ref.at[pl.ds(k * part, part)],
            sems.at[4 + k],
        )
        for k in range(PARTS)
    ]
    for c in slabs:
        c.start()
    for c in copies:
        c.wait()
    node = node_ref[...]
    weight = weight_ref[...]
    w16 = weight.astype(jnp.bfloat16).astype(jnp.float32)
    wy16 = (weight * label_ref[...]).astype(jnp.bfloat16).astype(jnp.float32)
    hot = lax.broadcasted_iota(jnp.int32, (nodes, node.shape[1]), 0) == node
    hot_ref[...] = jnp.where(hot, 1.0, 0.0).astype(jnp.bfloat16)
    sides = jnp.concatenate(
        [jnp.where(hot, w16, 0.0), jnp.where(hot, wy16, 0.0)], axis=0
    ).astype(jnp.bfloat16)
    sides_ref[...] = sides
    ones = jnp.ones((TILE, sides.shape[1]), jnp.bfloat16)
    total = lax.dot_general(
        ones, sides, (((1,), (1,)), ((), ())), preferred_element_type=jnp.float32
    )
    split = split_ref[...].astype(jnp.float32)
    held = split.shape[0] // groups
    packed = jnp.concatenate(
        [split[g * held : (g + 1) * held] for g in range(groups)], axis=1
    )
    if packed.shape[1] < LANES:
        packed = jnp.concatenate(
            [packed, jnp.zeros((held, LANES - packed.shape[1]), jnp.float32)], axis=1
        )
    block = jnp.concatenate([packed, total[:1]], axis=0)
    some = jnp.concatenate([block] * TILE, axis=0)
    for k in range(out_ref.shape[0] // some.shape[0]):
        out_ref[k * some.shape[0] : (k + 1) * some.shape[0]] = some
    for c in slabs:
        c.wait()


def partial_left(n_rows, n_feat, groups, held, feat_part, got_ref, bins_ref,
                 sides_ref, hot_ref, keep_ref, send_ref, total_ref):
    lines = held + 1
    layers = []
    for z in range(n_rows):
        cols = [
            got_ref[(z * n_feat + i) * lines : (z * n_feat + i) * lines + held]
            for i in range(n_feat)
        ]
        layers += [
            jnp.concatenate([c[:, g * feat_part : (g + 1) * feat_part] for c in cols], axis=1)
            for g in range(groups)
        ]
    splits = jnp.concatenate(layers, axis=0).astype(jnp.bfloat16)
    total_ref[...] = jnp.sum(
        got_ref[pl.ds(held, n_rows * n_feat, lines)], axis=0, keepdims=True
    )
    one, zero = jnp.bfloat16(1), jnp.bfloat16(0)
    rows, step = bins_ref.shape[0], 256
    left = jnp.zeros((sides_ref.shape[0], bins_ref.shape[1]), jnp.float32)
    for r in range(0, rows, step):
        row_split = lax.dot_general(
            hot_ref[:, r : r + step], splits, (((0,), (0,)), ((), ())),
            preferred_element_type=jnp.float32,
        )
        mask = jnp.where(
            bins_ref[r : r + step].astype(jnp.float32) <= row_split, 1.0, 0.0
        ).astype(jnp.bfloat16)
        left += jnp.dot(sides_ref[:, r : r + step], mask, preferred_element_type=jnp.float32)
    half = left.shape[1] // 2
    low, high = left[:, :half], left[:, half:]
    first = lax.axis_index("core") == 0
    keep_ref[...] = jnp.where(first, low, high)
    send_ref[...] = jnp.where(first, high, low)


def spread(n_rows, n_chip, half_n, keep_ref, recv_ref, out_ref):
    both = keep_ref[...] + recv_ref[...]
    nodes = both.shape[0] // 2
    for z in range(n_rows):
        for c in range(2):
            at = (z * 2 + c) * half_n
            tile = jnp.concatenate(
                [both[at : at + half_n], both[nodes + at : nodes + at + half_n]], axis=0
            )
            for chip in range(n_chip):
                out_ref[(z * n_chip + chip) * 2 + c] = tile


def split_gain(half_n, node_part, part_ref, total_ref, gain_ref):
    left = jnp.sum(part_ref[...], axis=0)
    left0 = jnp.concatenate([left[0, :half_n], left[1, :half_n]], axis=1)
    left1 = jnp.concatenate([left[0, half_n:], left[1, half_n:]], axis=1)
    row = total_ref[...]
    where = lax.axis_index("rows") * node_part + lax.axis_index("core") * half_n
    lane = lax.broadcasted_iota(jnp.int32, (half_n, LANES), 1)
    at = lax.broadcasted_iota(jnp.int32, (half_n, LANES), 0) + where
    total0 = jnp.sum(jnp.where(lane == at, row, 0.0), axis=1, keepdims=True)
    total1 = jnp.sum(jnp.where(lane == at + LANES // 2, row, 0.0), axis=1, keepdims=True)
    right0 = total0 - left0
    right1 = total1 - left1
    gain_ref[...] = (
        left1 * left1 / (left0 + 1.0)
        + right1 * right1 / (right0 + 1.0)
        - total1 * total1 / (total0 + 1.0)
    ) / (total0 + 1.0)


def finish(gain_ref, theirs_ref, out_ref, best_ref):
    mine, theirs = gain_ref[...], theirs_ref[...]
    first = lax.axis_index("core") == 0
    gain = jnp.concatenate(
        [jnp.where(first, mine, theirs), jnp.where(first, theirs, mine)], axis=0
    )
    n = gain.shape[0]
    best = jnp.max(gain, axis=1, keepdims=True)
    eye = lax.broadcasted_iota(jnp.int32, (n, n), 0) == lax.broadcasted_iota(jnp.int32, (n, n), 1)
    best_ref[...] = jnp.sum(jnp.where(eye, best, 0.0), axis=0, keepdims=True)
    feats, width = gain.shape[1], out_ref.shape[1]
    own = (lax.axis_index("chip") * 2 + lax.axis_index("core")) * width
    turned = pltpu.roll(gain, lax.rem(feats - own, feats), 1)
    out_ref[...] = turned[:, : out_ref.shape[1]]


def shards(bins, node_of, weight, label, split_bins):
    n_rows = lax.axis_size("rows")
    n_chip = lax.axis_size("chip")
    n_all = n_rows * n_chip * 2
    rows_here, feats = bins.shape
    node_part, feat_part = split_bins.shape
    nodes = node_part * n_rows
    half_f = feats // 2
    half_n = node_part // 2
    groups = min(LANES // feat_part, node_part)
    held = node_part // groups
    lines = held + 1

    per_row = [x.reshape(1, rows_here) for x in (node_of, weight, label)]
    def k_announce(*refs):
        announce(nodes, groups, lines, *refs)
    block, sides, hot, bins = call(
        k_announce,
        [f32(n_all * lines, LANES), bf16(2 * nodes, rows_here), bf16(nodes, rows_here),
         jax.ShapeDtypeStruct(bins.shape, jnp.int32)],
        bins, *per_row, split_bins, place=HBM,
        scratch=[
            pltpu.VMEM((1, rows_here), jnp.int32),
            pltpu.VMEM((1, rows_here), jnp.float32),
            pltpu.VMEM((1, rows_here), jnp.float32),
            pltpu.VMEM(split_bins.shape, jnp.int32),
            pltpu.SemaphoreType.DMA((4 + PARTS,)),
        ],
    )
    got = lax.all_to_all(
        block.reshape(n_all, 1, lines * LANES), ALL, 0, 0, tiled=True
    ).reshape(n_all * lines, LANES)

    def k_left(*refs):
        partial_left(n_rows, n_chip * 2, groups, held, feat_part, *refs)
    keep, send, total = call(
        k_left,
        [f32(2 * nodes, half_f), f32(2 * nodes, half_f), f32(1, LANES)],
        got, bins, sides, hot,
    )
    pair = [(0, 1), (1, 0)]
    recv = lax.ppermute(send, "core", pair)

    def k_spread(*refs):
        spread(n_rows, n_chip, half_n, *refs)
    (parts,) = call(k_spread, [f32(n_all, 2 * half_n, half_f)], keep, recv)
    parts = lax.all_to_all(parts, ALL, 0, 0, tiled=True)

    def k_gain(*refs):
        split_gain(half_n, node_part, *refs)
    (gain,) = call(
        k_gain, [f32(half_n, feats)],
        parts.reshape(n_all // 2, 2, 2 * half_n, half_f), total,
    )
    theirs = lax.ppermute(gain, "core", pair)
    out, best = call(
        finish, [f32(node_part, feat_part), f32(1, node_part)],
        gain, theirs,
    )
    return out, best.reshape(node_part)


def solution(mesh):
    n_rows, n_feat = mesh.devices.shape
    cores = Mesh(mesh.devices.reshape(n_rows, n_feat // 2, 2), ALL)
    placed = (P(ALL, None), P(ALL), P(ALL), P(ALL), P("rows", ("chip", "core")))
    return jax.shard_map(
        shards,
        mesh=cores,
        in_specs=placed,
        out_specs=(P("rows", ("chip", "core")), P("rows")),
        check_vma=False,
    )
```

time: 38.5 us -> 33.9 us (0.88)
  blocking collectives: 0 us -> 27 us
  waiting for transfers between devices: 20.3 us -> 2.3 us
  starting transfers between devices: 10.1 us -> 0.25 us
  other arithmetic: 3.4 us -> 0 us
  Pallas kernels: 0 us -> 3.38 us
  local copies, waits for them, and re-layouts: 2.64 us -> 0 us
  matrix products: 0.86 us -> 0 us
    all_to_all x0 -> x2, blocking collectives: none -> 27 us  [the longest x1 14.7 us: shards(): lax.all_to_all(block.reshape(n_all, 1, lines * LANES), ALL, 0, 0, tiled=T...]
    all_to_all x2 -> x0, waiting for transfers between devices: 18.1 us -> none  [the longest x1 10.5 us: shards(): parts = lax.all_to_all(parts, ALL, 0, 0, tiled=True)]
    all_to_all x2 -> x0, starting transfers between devices: 9.88 us -> none  [the longest x1 7.3 us: shards(): lax.all_to_all(jnp.broadcast_to(block[None], (n_all, block.shape[0])), AL...]
    pallas_call x0 -> x5, Pallas kernels: none -> 3.38 us  [call(): pl.pallas_call(kernel, out_shape=outs, in_specs=[place] * len(args), out_...]
    convert_element_type x2 -> x0, other arithmetic: 1.63 us -> none  [the longest x1 0.85 us: shards(): split_bins.reshape(-1).astype(jnp.float32)]
    broadcast_in_dim x2 -> x0, local copies, waits for them, and re-layouts: 1.39 us -> none  [the longest x1 0.72 us: shards(): jnp.broadcast_to(parts[:, None], (n_rows, n_chip, 2, 2, half_n, half_f))]
    dot_general x1 -> x0, matrix products: 0.86 us -> none  [shards(): left = jnp.dot(sides, mask, preferred_element_type=jnp.float32)]
    select_n x1 -> x0, other arithmetic: 0.78 us -> none  [shards(): jnp.where(node_hot, w16[None], zero)]
  transfers between devices with their start and end apart: 4 -> 2, of which waited for: 4 -> 2; matrix products, arithmetic and copies ran while one was open for 1% -> 0% of each run, Pallas kernels for 0% -> 0%
where the time goes in v2:
time: 33.9 us; the launch traced here: 33.6 us
  blocking collectives  27 us (80%)
  Pallas kernels  3.38 us (10%)
  waiting for transfers between devices  2.3 us (7%)
  between operations  0.67 us (2%)
    all_to_all x1, blocking collectives, shards(): lax.all_to_all(block.reshape(n_all, 1, lines * LANES), ALL, 0, 0, tiled=T...  14.7 us
    all_to_all x1, blocking collectives, shards(): parts = lax.all_to_all(parts, ALL, 0, 0, tiled=True)  12.3 us
    pallas_call x5, Pallas kernels, call(): pl.pallas_call(kernel, out_shape=outs, in_specs=[place] * len(args), out_...  3.38 us
    ppermute x1, waiting for transfers between devices, shards(): theirs = lax.ppermute(gain, 'core', pair)  1.16 us
    ppermute x1, waiting for transfers between devices, shards(): recv = lax.ppermute(send, 'core', pair)  1.14 us
  transfers between devices with their start and end apart: 2, of which 2 were waited for; matrix products, arithmetic and copies ran while one was open for 0% of the time, Pallas kernels for 0%

profile of v2, /device:TPU:0, one launch (start us, length us, event | category | flops | bytes accessed | tf_op | source)
XLA Modules:
  0.0 33.6 jit_solution(15681647462236523779)
XLA Ops:
  0.6 1.7 %shard_map.68 = (f32[160,128]{1,0:T(8,128)S(1)}, bf16[128,2048]{1,0:T(8,128)(2,1)S(1)}, bf16[64,2048]{1,0:T(8,128)(2,1)S(1)}, s32[2048,256]{1,0:T(8,128)S(1)}) custom-call(s32[2048,256]{1,0:T(8,128)} %refs_0_.1, s32[1,2048]{1,0:T(1,128)} %bitcast.10, f32[1,2048]{1,0:T(1,128)} %bitcast.11, f32[1,2048]{1,0:T(1,128)} %bitcast.12, s32[16,32]{1,0:T(8,128)} %refs_4_.1), custom_call_target="tpu_custom_call" | custom-call | bytes 5089280 | tf_op jit(solution)/shard_map/pallas_call | solution.py:20
  2.3 14.7 %all_to_all.10 = f32[32,1,640]{2,1,0:T(1,128)S(1)} all-to-all(f32[32,1,640]{2,1,0:T(1,128)S(1)} %bitcast.9), channel_id=1, replica_groups=mesh['rows'=4,'chip'=4,'core'=2] {'rows','chip','core'}, dimensions={0} | all-to-all | bytes 163840 | tf_op jit(solution)/shard_map/all_to_all | solution.py:206
  17.0 0.9 %shard_map.69 = (f32[128,128]{1,0:T(8,128)S(1)}, f32[128,128]{1,0:T(8,128)S(1)}, f32[1,128]{1,0:T(1,128)S(1)}) custom-call(f32[160,128]{1,0:T(8,128)S(1)} %bitcast.8, s32[2048,256]{1,0:T(8,128)S(1)} %get-tuple-element.12.refs_1_, bf16[128,2048]{1,0:T(8,128)(2,1)S(1)} %get-tuple-element.13.refs_2_, bf16[64,2048]{1,0:T(8,128)(2,1)S(1)} %get-tuple-element.14.refs_3_), custom_call_target="tpu_custom_call" | custom-call | bytes 3097088 | tf_op jit(solution)/shard_map/pallas_call | solution.py:20
  17.9 0.2 collective-permute-start
  18.1 1.1 %collective-permute-done.refs_1_ = f32[128,128]{1,0:T(8,128)S(1)} collective-permute-done((f32[128,128]{1,0:T(8,128)S(1)}, f32[128,128]{1,0:T(8,128)S(1)}, u32[]{:S(2)}, u32[]{:S(2)}) %collective-permute-start) | collective-permute-done | bytes 65568 | tf_op jit(solution)/shard_map/ppermute | solution.py:218
  19.3 12.3 %all_to_all.11 = f32[32,16,128]{2,1,0:T(8,128)S(1)} all-to-all(f32[32,16,128]{2,1,0:T(8,128)S(1)} %shard_map.70), channel_id=1, replica_groups=mesh['rows'=4,'chip'=4,'core'=2] {'rows','chip','core'}, dimensions={0} | all-to-all | bytes 524288 | tf_op jit(solution)/shard_map/all_to_all | solution.py:223
  31.6 0.1 shard_map.71.gain_ref
  31.7 0.1 collective-permute-start.1
  31.8 1.2 %collective-permute-done.1.theirs_ref = f32[8,256]{1,0:T(8,128)S(1)} collective-permute-done((f32[8,256]{1,0:T(8,128)S(1)}, f32[8,256]{1,0:T(8,128)S(1)}, u32[]{:S(2)}, u32[]{:S(2)}) %collective-permute-start.1) | collective-permute-done | bytes 8224 | tf_op jit(solution)/shard_map/ppermute | solution.py:231
  32.9 0.7 %shard_map.72 = (f32[16,32]{1,0:T(8,128)}, f32[1,16]{1,0:T(1,128)}) custom-call(f32[8,256]{1,0:T(8,128)S(1)} %shard_map.71.gain_ref, f32[8,256]{1,0:T(8,128)S(1)} %collective-permute-done.1.theirs_ref), custom_call_target="tpu_custom_call" | custom-call | bytes 18496 | tf_op jit(solution)/shard_map/pallas_call | solution.py:20
  (1 shorter events, 0.0 us)
Async XLA Ops:
  17.9 1.3 %collective-permute-start = (f32[128,128]{1,0:T(8,128)S(1)}, f32[128,128]{1,0:T(8,128)S(1)}, u32[]{:S(2)}, u32[]{:S(2)}) collective-permute-start(f32[128,128]{1,0:T(8,128)S(1)} %get-tuple-element.16), channel_id=1, source_target_pairs={{0,1},{1,0},{2,3},{3,2},{4,5},{5,4},{6,7},{7,6},{8,9},{9,8},{10,11... | collective-permute-start | bytes 196616 | tf_op jit(solution)/shard_map/ppermute | solution.py:218
  31.7 1.2 %collective-permute-start.1 = (f32[8,256]{1,0:T(8,128)S(1)}, f32[8,256]{1,0:T(8,128)S(1)}, u32[]{:S(2)}, u32[]{:S(2)}) collective-permute-start(f32[8,256]{1,0:T(8,128)S(1)} %shard_map.71.gain_ref), channel_id=1, source_target_pairs={{0,1},{1,0},{2,3},{3,2},{4,5},{5,4},{6,7},{7,6},{8,9},{9,8},{10,11... | collective-permute-start | bytes 24584 | tf_op jit(solution)/shard_map/ppermute | solution.py:231

commit v3 on v2

v3 whole, which is shorter than its diff:
```python
import math

import jax
import jax.numpy as jnp
from jax import lax
from jax.experimental import pallas as pl
from jax.experimental.pallas import tpu as pltpu
from jax.sharding import Mesh, PartitionSpec as P

ALL = ("rows", "line", "chip", "core")
FIRST = ("rows", "line", "chip", "core")
SECOND = ("line", "chip", "core", "rows")
LANES = 128
BINS = 16
PARTS = 4
STEP = 512
VMEM = pl.BlockSpec(memory_space=pltpu.VMEM)
HBM = pl.BlockSpec(memory_space=pltpu.HBM)
ANY = pl.BlockSpec(memory_space=pl.ANY)


def place_in(order, sizes, **at):
    d = 0
    for axis in order:
        d = d * sizes[axis] + at[axis]
    return d


def call(kernel, outs, *args, place=None, scratch=()):
    place = place or [VMEM] * len(args)
    args = [
        pltpu.with_memory_space_constraint(x, pltpu.HBM) if p is HBM else x
        for x, p in zip(args, place)
    ]
    size = sum(x.size * x.dtype.itemsize for x in (*args, *outs))
    return pl.pallas_call(
        kernel,
        out_shape=outs,
        in_specs=place,
        out_specs=tuple([VMEM] * len(outs)),
        scratch_shapes=list(scratch),
        compiler_params=pltpu.CompilerParams(vmem_limit_bytes=16 << 20),
        cost_estimate=pl.CostEstimate(flops=0, bytes_accessed=size, transcendentals=0),
    )(*args)


def f32(*shape):
    return jax.ShapeDtypeStruct(shape, jnp.float32)


def announce(groups, node_hbm, weight_hbm, label_hbm, split_hbm, out_ref, row_ref,
             node_ref, weight_ref, label_ref, split_ref, sems):
    copies = [
        pltpu.make_async_copy(src, dst, sems.at[k])
        for k, (src, dst) in enumerate(
            ((split_hbm, split_ref), (node_hbm, node_ref), (weight_hbm, weight_ref),
             (label_hbm, label_ref))
        )
    ]
    for c in copies:
        c.start()
    for c in copies:
        c.wait()
    split = split_ref[...].astype(jnp.float32)
    held = split.shape[0] // groups
    block = jnp.concatenate(
        [split[g * held : (g + 1) * held] for g in range(groups)], axis=1
    )
    if block.shape[1] < LANES:
        block = jnp.concatenate(
            [block, jnp.zeros((held, LANES - block.shape[1]), jnp.float32)], axis=1
        )
    many = max(1, 8 // held)
    some = jnp.concatenate([block] * many, axis=0)
    for k in range(out_ref.shape[0] // some.shape[0]):
        out_ref[k * some.shape[0] : (k + 1) * some.shape[0]] = some
    weight = weight_ref[...]
    row_ref[0:1] = node_ref[...].astype(jnp.float32)
    row_ref[1:2] = weight.astype(jnp.bfloat16).astype(jnp.float32)
    row_ref[2:3] = (weight * label_ref[...]).astype(jnp.bfloat16).astype(jnp.float32)


def histogram(nodes, bins_hbm, row_ref, far_bins, far_row, out_ref, bins_ref, sems):
    rows, half = bins_ref.shape
    part = rows // PARTS
    first = pl.multiple_of(lax.axis_index("core") * half, half)
    copies = [
        pltpu.make_async_copy(
            bins_hbm.at[pl.ds(k * part, part), pl.ds(first, half)],
            bins_ref.at[pl.ds(k * part, part)],
            sems.at[k],
        )
        for k in range(PARTS)
    ]
    for c in copies:
        c.start()

    def sides_of(ref):
        node = ref[0:1].astype(jnp.int32)
        hot = lax.broadcasted_iota(jnp.int32, (nodes, rows), 0) == node
        return jnp.concatenate(
            [jnp.where(hot, ref[1:2], 0.0), jnp.where(hot, ref[2:3], 0.0)], axis=0
        ).astype(jnp.bfloat16)

    def add(sides, bins, seed):
        one, zero = jnp.bfloat16(1), jnp.bfloat16(0)
        for b in range(0, BINS, 2):
            acc = jnp.zeros((2 * nodes, 2 * half), jnp.float32)
            for r in range(0, rows, STEP):
                chunk = bins[r : r + STEP]
                mask = jnp.concatenate(
                    [jnp.where(chunk <= jnp.bfloat16(b + k), one, zero) for k in range(2)],
                    axis=1,
                )
                acc += jnp.dot(
                    sides[:, r : r + STEP], mask, preferred_element_type=jnp.float32
                )
            for k in range(2):
                here = acc[:, k * half : (k + 1) * half]
                out_ref[b + k] = here if seed else out_ref[b + k] + here

    add(sides_of(far_row), far_bins[:, pl.ds(first, half)].astype(jnp.bfloat16), True)
    sides = sides_of(row_ref)
    for c in copies:
        c.wait()
    add(sides, bins_ref[...].astype(jnp.bfloat16), False)


def choose(sizes, groups, held, feat_part, half_n, got_ref, below_ref, out_ref):
    half = below_ref.shape[2]
    nodes = below_ref.shape[1] // 2
    mine = half // feat_part
    base = lax.axis_index("core") * mine
    n_rows, n_line, n_chip = sizes["rows"], sizes["line"], sizes["chip"]
    layers = []
    for z in range(n_rows):
        cols = []
        for i in range(mine):
            chip = (base + i) // 2
            d = place_in(
                FIRST, sizes, rows=z, line=chip // n_chip, chip=chip % n_chip, core=i % 2
            )
            cols.append(got_ref[pl.ds(d * held, held)])
        layers += [
            jnp.concatenate([c[:, g * feat_part : (g + 1) * feat_part] for c in cols], axis=1)
            for g in range(groups)
        ]
    split = jnp.concatenate(layers, axis=0)
    left0, left1 = below_ref[0, :nodes], below_ref[0, nodes:]
    for b in range(1, BINS - 1):
        further = split >= b
        left0 = jnp.where(further, below_ref[b, :nodes], left0)
        left1 = jnp.where(further, below_ref[b, nodes:], left1)
    everything = below_ref[BINS - 1]
    eye = lax.broadcasted_iota(jnp.int32, everything.shape, 0) == lax.broadcasted_iota(
        jnp.int32, everything.shape, 1
    )
    total = jnp.sum(jnp.where(eye, everything, 0.0), axis=0, keepdims=True)
    lines = 2 * half_n + 1
    for z in range(n_rows):
        for c in range(2):
            at = (z * 2 + c) * half_n
            tile = jnp.concatenate(
                [left0[at : at + half_n], left1[at : at + half_n], total], axis=0
            )
            for line in range(n_line):
                for chip in range(n_chip):
                    d = place_in(SECOND, sizes, rows=z, line=line, chip=chip, core=c)
                    out_ref[d * lines : (d + 1) * lines] = tile


def split_gain(half_n, node_part, sizes, part_ref, gain_ref):
    lines = 2 * half_n + 1
    sums = []
    for c in range(2):
        both = None
        for z in range(sizes["rows"]):
            for line in range(sizes["line"]):
                for chip in range(sizes["chip"]):
                    d = place_in(SECOND, sizes, rows=z, line=line, chip=chip, core=c)
                    one = part_ref[d * lines : (d + 1) * lines]
                    both = one if both is None else both + one
        sums.append(both)
    left0 = jnp.concatenate([s[:half_n] for s in sums], axis=1)
    left1 = jnp.concatenate([s[half_n : 2 * half_n] for s in sums], axis=1)
    row = sums[0][2 * half_n :]
    where = lax.axis_index("rows") * node_part + lax.axis_index("core") * half_n
    lane = lax.broadcasted_iota(jnp.int32, (half_n, LANES), 1)
    at = lax.broadcasted_iota(jnp.int32, (half_n, LANES), 0) + where
    total0 = jnp.sum(jnp.where(lane == at, row, 0.0), axis=1, keepdims=True)
    total1 = jnp.sum(jnp.where(lane == at + LANES // 2, row, 0.0), axis=1, keepdims=True)
    right0 = total0 - left0
    right1 = total1 - left1
    gain_ref[...] = (
        left1 * left1 / (left0 + 1.0)
        + right1 * right1 / (right0 + 1.0)
        - total1 * total1 / (total0 + 1.0)
    ) / (total0 + 1.0)


def finish(gain_ref, theirs_ref, out_ref, best_ref):
    mine, theirs = gain_ref[...], theirs_ref[...]
    first = lax.axis_index("core") == 0
    gain = jnp.concatenate(
        [jnp.where(first, mine, theirs), jnp.where(first, theirs, mine)], axis=0
    )
    n = gain.shape[0]
    best = jnp.max(gain, axis=1, keepdims=True)
    eye = lax.broadcasted_iota(jnp.int32, (n, n), 0) == lax.broadcasted_iota(jnp.int32, (n, n), 1)
    best_ref[...] = jnp.sum(jnp.where(eye, best, 0.0), axis=0, keepdims=True)
    feats, width = gain.shape[1], out_ref.shape[1]
    own = lax.axis_index(("line", "chip", "core")) * width
    turned = pltpu.roll(gain, lax.rem(feats - own, feats), 1)
    out_ref[...] = turned[:, : out_ref.shape[1]]


def shards(bins, node_of, weight, label, split_bins):
    sizes = {axis: lax.axis_size(axis) for axis in ALL}
    n_rows = sizes["rows"]
    n_all = math.prod(sizes.values())
    rows_here, feats = bins.shape
    node_part, feat_part = split_bins.shape
    nodes = node_part * n_rows
    half_f = feats // 2
    half_n = node_part // 2
    groups = min(LANES // feat_part, node_part)
    held = node_part // groups
    lines = 2 * half_n + 1
    pair = [(0, 1), (1, 0)]
    far_bins = lax.ppermute(bins, "core", pair)
    def k_announce(*refs):
        announce(groups, *refs)
    per_row = [x.reshape(1, rows_here) for x in (node_of, weight, label)]
    block, row = call(
        k_announce, [f32(n_all * held, LANES), f32(3, rows_here)], *per_row, split_bins,
        place=[HBM] * 4,
        scratch=[
            pltpu.VMEM((1, rows_here), jnp.int32),
            pltpu.VMEM((1, rows_here), jnp.float32),
            pltpu.VMEM((1, rows_here), jnp.float32),
            pltpu.VMEM(split_bins.shape, jnp.int32),
            pltpu.SemaphoreType.DMA((4,)),
        ],
    )
    got = lax.all_to_all(
        block.reshape(n_all, 1, held * LANES), FIRST, 0, 0, tiled=True
    ).reshape(n_all * held, LANES)
    far_row = lax.ppermute(row, "core", pair)

    def k_histogram(*refs):
        histogram(nodes, *refs)
    (below,) = call(
        k_histogram, [f32(BINS, 2 * nodes, half_f)], bins, row, far_bins, far_row,
        place=[HBM, VMEM, VMEM, VMEM],
        scratch=[pltpu.VMEM((rows_here, half_f), jnp.int32), pltpu.SemaphoreType.DMA((PARTS,))],
    )

    def k_choose(*refs):
        choose(sizes, groups, held, feat_part, half_n, *refs)
    (parts,) = call(k_choose, [f32(n_all * lines, half_f)], got, below)
    parts = lax.all_to_all(
        parts.reshape(n_all, 1, lines * half_f), SECOND, 0, 0, tiled=True
    ).reshape(n_all * lines, half_f)

    def k_gain(*refs):
        split_gain(half_n, node_part, sizes, *refs)
    (gain,) = call(k_gain, [f32(half_n, feats)], parts)
    other = lax.ppermute(gain, "core", pair)
    out, best = call(
        finish, [f32(node_part, feat_part), f32(1, node_part)], gain, other
    )
    return out, best.reshape(node_part)


def solution(mesh):
    n_rows, n_feat = mesh.devices.shape
    cores = Mesh(mesh.devices.reshape(n_rows, n_feat // 4, 2, 2), ALL)
    placed = (P(ALL, None), P(ALL), P(ALL), P(ALL), P("rows", ("line", "chip", "core")))
    return jax.shard_map(
        shards,
        mesh=cores,
        in_specs=placed,
        out_specs=(P("rows", ("line", "chip", "core")), P("rows")),
        check_vma=False,
    )
```

time: 33.9 us -> 32.2 us (0.950)
  blocking collectives: 27 us -> 12.5 us
  starting transfers between devices: 0.25 us -> 8.35 us
  waiting for transfers between devices: 2.3 us -> 5.39 us
  Pallas kernels: 3.38 us -> 5 us
    all_to_all x2 -> x1, blocking collectives: 27 us -> 12.5 us  [shards(): lax.all_to_all(parts.reshape(n_all, 1, lines * half_f), SECOND, 0, 0, til...]
    all_to_all x0 -> x1, starting transfers between devices: none -> 6.97 us  [shards(): lax.all_to_all(block.reshape(n_all, 1, held * LANES), FIRST, 0, 0, tiled=...]
    all_to_all x0 -> x1, waiting for transfers between devices: none -> 3.6 us  [shards(): lax.all_to_all(block.reshape(n_all, 1, held * LANES), FIRST, 0, 0, tiled=...]
    pallas_call x5, Pallas kernels: 3.38 us -> 5 us  [call(): pl.pallas_call(kernel, out_shape=outs, in_specs=place, out_specs=tuple([V...]
    ppermute x2 -> x3, starting transfers between devices: 0.25 us -> 1.39 us  [the longest x1 0.55 us: shards(): other = lax.ppermute(gain, 'core', pair)]
    ppermute x2 -> x3, waiting for transfers between devices: 2.3 us -> 1.79 us  [the longest x1 0.96 us: shards(): far_row = lax.ppermute(row, 'core', pair)]
  transfers between devices with their start and end apart: 2 -> 4, of which waited for: 2 -> 3; matrix products, arithmetic and copies ran while one was open for 0% -> 0% of each run, Pallas kernels for 0% -> 13%
where the time goes in v3:
time: 32.2 us; the launch traced here: 31.9 us
  blocking collectives  12.5 us (39%)
  starting transfers between devices  8.35 us (26%)
  waiting for transfers between devices  5.39 us (17%)
  Pallas kernels  5 us (16%)
  between operations  0.67 us (2%)
    all_to_all x1, blocking collectives, shards(): lax.all_to_all(parts.reshape(n_all, 1, lines * half_f), SECOND, 0, 0, til...  12.5 us
    all_to_all x1, starting transfers between devices, shards(): lax.all_to_all(block.reshape(n_all, 1, held * LANES), FIRST, 0, 0, tiled=...  6.97 us
    pallas_call x5, Pallas kernels, call(): pl.pallas_call(kernel, out_shape=outs, in_specs=place, out_specs=tuple([V...  5 us
    all_to_all x1, waiting for transfers between devices, shards(): lax.all_to_all(block.reshape(n_all, 1, held * LANES), FIRST, 0, 0, tiled=...  3.6 us
    ppermute x1, waiting for transfers between devices, shards(): far_row = lax.ppermute(row, 'core', pair)  0.96 us
    ppermute x1, waiting for transfers between devices, shards(): other = lax.ppermute(gain, 'core', pair)  0.83 us
  transfers between devices with their start and end apart: 4, of which 3 were waited for; matrix products, arithmetic and copies ran while one was open for 0% of the time, Pallas kernels for 13%

profile of v3, /device:TPU:0, one launch (start us, length us, event | category | flops | bytes accessed | tf_op | source)
XLA Modules:
  0.0 31.9 jit_solution(17671619051321169094)
XLA Ops:
  0.6 0.5 %collective-permute-start = (s32[2048,256]{1,0:T(8,128)}, s32[2048,256]{1,0:T(8,128)S(1)}, u32[]{:S(2)}, u32[]{:S(2)}) collective-permute-start(s32[2048,256]{1,0:T(8,128)} %refs_0_.1), channel_id=1, source_target_pairs={{0,1},{1,0},{2,3},{3,2},{4,5},{5,4},{6,7},{7,6},{8,9},{9,8},{10,11... | collective-permute-start | bytes 6291464 | tf_op jit(solution)/shard_map/ppermute | solution.py:230
  1.1 1.5 %shard_map.68 = (f32[128,128]{1,0:T(8,128)}, f32[3,2048]{1,0:T(4,128)S(1)}) custom-call(s32[1,2048]{1,0:T(1,128)} %bitcast.11, f32[1,2048]{1,0:T(1,128)} %bitcast.12, f32[1,2048]{1,0:T(1,128)} %bitcast.13, s32[16,32]{1,0:T(8,128)} %refs_3_.1), custom_call_target="tpu_custom_call" | custom-call | bytes 116736 | tf_op jit(solution)/shard_map/pallas_call | solution.py:36
  2.7 7.0 %all-to-all-start = ((f32[32,1,512]{2,1,0:T(1,128)}), f32[32,1,512]{2,1,0:T(1,128)S(1)}, u32[]{:S(2)}, u32[]{:S(2)}) async-start(f32[32,1,512]{2,1,0:T(1,128)} %bitcast.3), calls=%async_computation | async-start | bytes 131072 | tf_op jit(solution)/shard_map/all_to_all | solution.py:245
  9.6 0.3 collective-permute-start.1
  9.9 1.0 %collective-permute-done.1.refs_3_ = f32[3,2048]{1,0:T(4,128)S(1)} collective-permute-done((f32[3,2048]{1,0:T(4,128)S(1)}, f32[3,2048]{1,0:T(4,128)S(1)}, u32[]{:S(2)}, u32[]{:S(2)}) %collective-permute-start.1) | collective-permute-done | bytes 24608 | tf_op jit(solution)/shard_map/ppermute | solution.py:248
  10.9 0.0 collective-permute-done.refs_2_
  10.9 2.5 %shard_map.69.refs_1_ = f32[16,128,128]{2,1,0:T(8,128)S(1)} custom-call(s32[2048,256]{1,0:T(8,128)} %refs_0_.1, f32[3,2048]{1,0:T(4,128)S(1)} %get-tuple-element.7.refs_1_, s32[2048,256]{1,0:T(8,128)S(1)} %collective-permute-done.refs_2_, f32[3,2048]{1,0:T(4,128)S(1)} %collective-permute-done.1.refs_3_), custom_call_target="tpu_custom_call" | custom-call | bytes 5292032 | tf_op jit(solution)/shard_map/pallas_call | solution.py:36
  13.4 3.6 %all-to-all-done = f32[32,1,512]{2,1,0:T(1,128)S(1)} async-done(((f32[32,1,512]{2,1,0:T(1,128)}), f32[32,1,512]{2,1,0:T(1,128)S(1)}, u32[]{:S(2)}, u32[]{:S(2)}) %all-to-all-start) | async-done | bytes 65568 | tf_op jit(solution)/shard_map/all_to_all | solution.py:245
  17.0 0.2 shard_map.70
  17.2 12.5 %all_to_all.10 = f32[32,1,2176]{2,1,0:T(1,128)S(1)} all-to-all(f32[32,1,2176]{2,1,0:T(1,128)S(1)} %bitcast.8), channel_id=1, replica_groups=mesh['rows'=4,'line'=2,'chip'=2,'core'=2] {'line','chip','core','rows'}, dimensions={0} | all-to-all | bytes 557056 | tf_op jit(solution)/shard_map/all_to_all | solution.py:261
  29.7 0.1 shard_map.71.gain_ref
  29.8 0.6 %collective-permute-start.2 = (f32[8,256]{1,0:T(8,128)S(1)}, f32[8,256]{1,0:T(8,128)S(1)}, u32[]{:S(2)}, u32[]{:S(2)}) collective-permute-start(f32[8,256]{1,0:T(8,128)S(1)} %shard_map.71.gain_ref), channel_id=1, source_target_pairs={{0,1},{1,0},{2,3},{3,2},{4,5},{5,4},{6,7},{7,6},{8,9},{9,8},{10,11... | collective-permute-start | bytes 24584 | tf_op jit(solution)/shard_map/ppermute | solution.py:268
  30.4 0.8 %collective-permute-done.2.theirs_ref = f32[8,256]{1,0:T(8,128)S(1)} collective-permute-done((f32[8,256]{1,0:T(8,128)S(1)}, f32[8,256]{1,0:T(8,128)S(1)}, u32[]{:S(2)}, u32[]{:S(2)}) %collective-permute-start.2) | collective-permute-done | bytes 8224 | tf_op jit(solution)/shard_map/ppermute | solution.py:268
  31.2 0.7 %shard_map.72 = (f32[16,32]{1,0:T(8,128)}, f32[1,16]{1,0:T(1,128)}) custom-call(f32[8,256]{1,0:T(8,128)S(1)} %shard_map.71.gain_ref, f32[8,256]{1,0:T(8,128)S(1)} %collective-permute-done.2.theirs_ref), custom_call_target="tpu_custom_call" | custom-call | bytes 18496 | tf_op jit(solution)/shard_map/pallas_call | solution.py:36
Async XLA Ops:
  0.6 10.3 %collective-permute-start = (s32[2048,256]{1,0:T(8,128)}, s32[2048,256]{1,0:T(8,128)S(1)}, u32[]{:S(2)}, u32[]{:S(2)}) collective-permute-start(s32[2048,256]{1,0:T(8,128)} %refs_0_.1), channel_id=1, source_target_pairs={{0,1},{1,0},{2,3},{3,2},{4,5},{5,4},{6,7},{7,6},{8,9},{9,8},{10,11... | collective-permute-start | bytes 6291464 | tf_op jit(solution)/shard_map/ppermute | solution.py:230
  2.7 14.4 %all-to-all-start = ((f32[32,1,512]{2,1,0:T(1,128)}), f32[32,1,512]{2,1,0:T(1,128)S(1)}, u32[]{:S(2)}, u32[]{:S(2)}) async-start(f32[32,1,512]{2,1,0:T(1,128)} %bitcast.3), calls=%async_computation | async-start | bytes 131072 | tf_op jit(solution)/shard_map/all_to_all | solution.py:245
  9.6 1.3 %collective-permute-start.1 = (f32[3,2048]{1,0:T(4,128)S(1)}, f32[3,2048]{1,0:T(4,128)S(1)}, u32[]{:S(2)}, u32[]{:S(2)}) collective-permute-start(f32[3,2048]{1,0:T(4,128)S(1)} %get-tuple-element.7.refs_1_), channel_id=1, source_target_pairs={{0,1},{1,0},{2,3},{3,2},{4,5},{5,4},{6,7},{7,6},{8,9},{9,8},{10,11... | collective-permute-start | bytes 73736 | tf_op jit(solution)/shard_map/ppermute | solution.py:248
  29.8 1.4 %collective-permute-start.2 = (f32[8,256]{1,0:T(8,128)S(1)}, f32[8,256]{1,0:T(8,128)S(1)}, u32[]{:S(2)}, u32[]{:S(2)}) collective-permute-start(f32[8,256]{1,0:T(8,128)S(1)} %shard_map.71.gain_ref), channel_id=1, source_target_pairs={{0,1},{1,0},{2,3},{3,2},{4,5},{5,4},{6,7},{7,6},{8,9},{9,8},{10,11... | collective-permute-start | bytes 24584 | tf_op jit(solution)/shard_map/ppermute | solution.py:268

commit v4 on v3

--- a/solution.py
+++ b/solution.py
@@ -7,9 +7,11 @@
 from jax.experimental.pallas import tpu as pltpu
 from jax.sharding import Mesh, PartitionSpec as P
 
-ALL = ("rows", "line", "chip", "core")
-FIRST = ("rows", "line", "chip", "core")
-SECOND = ("line", "chip", "core", "rows")
+ROWS = ("far", "near")
+FEAT = ("line", "chip", "core")
+ALL = ROWS + FEAT
+FIRST = ("far", "near", "line", "chip", "core")
+SECOND = ("core", "near", "line", "chip", "far")
 LANES = 128
 BINS = 16
 PARTS = 4
@@ -26,7 +28,7 @@
     return d
 
 
-def call(kernel, outs, *args, place=None, scratch=()):
+def call(kernel, outs, *args, place=None, where=None, scratch=()):
     place = place or [VMEM] * len(args)
     args = [
         pltpu.with_memory_space_constraint(x, pltpu.HBM) if p is HBM else x
@@ -37,7 +39,7 @@
         kernel,
         out_shape=outs,
         in_specs=place,
-        out_specs=tuple([VMEM] * len(outs)),
+        out_specs=tuple(where or [VMEM] * len(outs)),
         scratch_shapes=list(scratch),
         compiler_params=pltpu.CompilerParams(vmem_limit_bytes=16 << 20),
         cost_estimate=pl.CostEstimate(flops=0, bytes_accessed=size, transcendentals=0),
@@ -49,7 +51,7 @@
 
 
 def announce(groups, node_hbm, weight_hbm, label_hbm, split_hbm, out_ref, row_ref,
-             node_ref, weight_ref, label_ref, split_ref, sems):
+             node_ref, weight_ref, label_ref, split_ref, block_ref, sems):
     copies = [
         pltpu.make_async_copy(src, dst, sems.at[k])
         for k, (src, dst) in enumerate(
@@ -59,8 +61,7 @@
     ]
     for c in copies:
         c.start()
-    for c in copies:
-        c.wait()
+    copies[0].wait()
     split = split_ref[...].astype(jnp.float32)
     held = split.shape[0] // groups
     block = jnp.concatenate(
@@ -72,12 +73,17 @@
         )
     many = max(1, 8 // held)
     some = jnp.concatenate([block] * many, axis=0)
-    for k in range(out_ref.shape[0] // some.shape[0]):
-        out_ref[k * some.shape[0] : (k + 1) * some.shape[0]] = some
+    for k in range(block_ref.shape[0] // some.shape[0]):
+        block_ref[k * some.shape[0] : (k + 1) * some.shape[0]] = some
+    out = pltpu.make_async_copy(block_ref, out_ref, sems.at[4])
+    out.start()
+    for c in copies[1:]:
+        c.wait()
     weight = weight_ref[...]
     row_ref[0:1] = node_ref[...].astype(jnp.float32)
     row_ref[1:2] = weight.astype(jnp.bfloat16).astype(jnp.float32)
     row_ref[2:3] = (weight * label_ref[...]).astype(jnp.bfloat16).astype(jnp.float32)
+    out.wait()
 
 
 def histogram(nodes, bins_hbm, row_ref, far_bins, far_row, out_ref, bins_ref, sems):
@@ -131,14 +137,16 @@
     nodes = below_ref.shape[1] // 2
     mine = half // feat_part
     base = lax.axis_index("core") * mine
-    n_rows, n_line, n_chip = sizes["rows"], sizes["line"], sizes["chip"]
+    n_near, n_line, n_chip = sizes["near"], sizes["line"], sizes["chip"]
+    n_rows = sizes["far"] * n_near
     layers = []
     for z in range(n_rows):
         cols = []
         for i in range(mine):
             chip = (base + i) // 2
             d = place_in(
-                FIRST, sizes, rows=z, line=chip // n_chip, chip=chip % n_chip, core=i % 2
+                FIRST, sizes, far=z // n_near, near=z % n_near,
+                line=chip // n_chip, chip=chip % n_chip, core=i % 2,
             )
             cols.append(got_ref[pl.ds(d * held, held)])
         layers += [
@@ -165,26 +173,28 @@
             )
             for line in range(n_line):
                 for chip in range(n_chip):
-                    d = place_in(SECOND, sizes, rows=z, line=line, chip=chip, core=c)
+                    d = place_in(
+                        SECOND, sizes, far=z // n_near, near=z % n_near,
+                        line=line, chip=chip, core=c,
+                    )
                     out_ref[d * lines : (d + 1) * lines] = tile
 
 
 def split_gain(half_n, node_part, sizes, part_ref, gain_ref):
     lines = 2 * half_n + 1
+    after = math.prod(sizes[a] for a in SECOND[SECOND.index("core") + 1 :])
     sums = []
     for c in range(2):
         both = None
-        for z in range(sizes["rows"]):
-            for line in range(sizes["line"]):
-                for chip in range(sizes["chip"]):
-                    d = place_in(SECOND, sizes, rows=z, line=line, chip=chip, core=c)
-                    one = part_ref[d * lines : (d + 1) * lines]
-                    both = one if both is None else both + one
+        for d in range(math.prod(sizes.values())):
+            if (d // after) % 2 == c:
+                one = part_ref[d * lines : (d + 1) * lines]
+                both = one if both is None else both + one
         sums.append(both)
     left0 = jnp.concatenate([s[:half_n] for s in sums], axis=1)
     left1 = jnp.concatenate([s[half_n : 2 * half_n] for s in sums], axis=1)
     row = sums[0][2 * half_n :]
-    where = lax.axis_index("rows") * node_part + lax.axis_index("core") * half_n
+    where = lax.axis_index(ROWS) * node_part + lax.axis_index("core") * half_n
     lane = lax.broadcasted_iota(jnp.int32, (half_n, LANES), 1)
     at = lax.broadcasted_iota(jnp.int32, (half_n, LANES), 0) + where
     total0 = jnp.sum(jnp.where(lane == at, row, 0.0), axis=1, keepdims=True)
@@ -209,14 +219,14 @@
     eye = lax.broadcasted_iota(jnp.int32, (n, n), 0) == lax.broadcasted_iota(jnp.int32, (n, n), 1)
     best_ref[...] = jnp.sum(jnp.where(eye, best, 0.0), axis=0, keepdims=True)
     feats, width = gain.shape[1], out_ref.shape[1]
-    own = lax.axis_index(("line", "chip", "core")) * width
+    own = lax.axis_index(FEAT) * width
     turned = pltpu.roll(gain, lax.rem(feats - own, feats), 1)
     out_ref[...] = turned[:, : out_ref.shape[1]]
 
 
 def shards(bins, node_of, weight, label, split_bins):
     sizes = {axis: lax.axis_size(axis) for axis in ALL}
-    n_rows = sizes["rows"]
+    n_rows = sizes["far"] * sizes["near"]
     n_all = math.prod(sizes.values())
     rows_here, feats = bins.shape
     node_part, feat_part = split_bins.shape
@@ -233,13 +243,14 @@
     per_row = [x.reshape(1, rows_here) for x in (node_of, weight, label)]
     block, row = call(
         k_announce, [f32(n_all * held, LANES), f32(3, rows_here)], *per_row, split_bins,
-        place=[HBM] * 4,
+        place=[HBM] * 4, where=[HBM, VMEM],
         scratch=[
             pltpu.VMEM((1, rows_here), jnp.int32),
             pltpu.VMEM((1, rows_here), jnp.float32),
             pltpu.VMEM((1, rows_here), jnp.float32),
             pltpu.VMEM(split_bins.shape, jnp.int32),
-            pltpu.SemaphoreType.DMA((4,)),
+            pltpu.VMEM((n_all * held, LANES), jnp.float32),
+            pltpu.SemaphoreType.DMA((5,)),
         ],
     )
     got = lax.all_to_all(
@@ -274,12 +285,12 @@
 
 def solution(mesh):
     n_rows, n_feat = mesh.devices.shape
-    cores = Mesh(mesh.devices.reshape(n_rows, n_feat // 4, 2, 2), ALL)
-    placed = (P(ALL, None), P(ALL), P(ALL), P(ALL), P("rows", ("line", "chip", "core")))
+    cores = Mesh(mesh.devices.reshape(n_rows // 2, 2, n_feat // 4, 2, 2), ALL)
+    placed = (P(ALL, None), P(ALL), P(ALL), P(ALL), P(ROWS, FEAT))
     return jax.shard_map(
         shards,
         mesh=cores,
         in_specs=placed,
-        out_specs=(P("rows", ("line", "chip", "core")), P("rows")),
+        out_specs=(P(ROWS, FEAT), P(ROWS)),
         check_vma=False,
     )

time: 32.2 us -> 31.6 us (0.981)
  blocking collectives: 12.5 us -> 12.1 us
    all_to_all x1, blocking collectives: 12.5 us -> 12.1 us  [shards(): lax.all_to_all(parts.reshape(n_all, 1, lines * half_f), SECOND, 0, 0, til...]
where the time goes in v4:
time: 31.6 us; the launch traced here: 31.3 us
  blocking collectives  12.1 us (38%)
  starting transfers between devices  8.12 us (26%)
  waiting for transfers between devices  5.47 us (17%)
  Pallas kernels  4.94 us (16%)
  between operations  0.67 us (2%)
    all_to_all x1, blocking collectives, shards(): lax.all_to_all(parts.reshape(n_all, 1, lines * half_f), SECOND, 0, 0, til...  12.1 us
    all_to_all x1, starting transfers between devices, shards(): lax.all_to_all(block.reshape(n_all, 1, held * LANES), FIRST, 0, 0, tiled=...  6.97 us
    pallas_call x5, Pallas kernels, call(): pl.pallas_call(kernel, out_shape=outs, in_specs=place, out_specs=tuple(wh...  4.94 us
    all_to_all x1, waiting for transfers between devices, shards(): lax.all_to_all(block.reshape(n_all, 1, held * LANES), FIRST, 0, 0, tiled=...  3.6 us
    ppermute x1, waiting for transfers between devices, shards(): far_row = lax.ppermute(row, 'core', pair)  0.96 us
    ppermute x1, waiting for transfers between devices, shards(): other = lax.ppermute(gain, 'core', pair)  0.92 us
  transfers between devices with their start and end apart: 4, of which 3 were waited for; matrix products, arithmetic and copies ran while one was open for 0% of the time, Pallas kernels for 13%

profile of v4, /device:TPU:0, one launch (start us, length us, event | category | flops | bytes accessed | tf_op | source)
XLA Modules:
  0.0 31.3 jit_solution(8527227764181325198)
XLA Ops:
  0.6 0.5 %collective-permute-start = (s32[2048,256]{1,0:T(8,128)}, s32[2048,256]{1,0:T(8,128)S(1)}, u32[]{:S(2)}, u32[]{:S(2)}) collective-permute-start(s32[2048,256]{1,0:T(8,128)} %refs_0_.1), channel_id=1, source_target_pairs={{0,1},{1,0},{2,3},{3,2},{4,5},{5,4},{6,7},{7,6},{8,9},{9,8},{10,11... | collective-permute-start | bytes 6291464 | tf_op jit(solution)/shard_map/ppermute | solution.py:240
  1.1 1.4 %shard_map.68 = (f32[128,128]{1,0:T(8,128)}, f32[3,2048]{1,0:T(4,128)S(1)}) custom-call(s32[1,2048]{1,0:T(1,128)} %bitcast.11, f32[1,2048]{1,0:T(1,128)} %bitcast.12, f32[1,2048]{1,0:T(1,128)} %bitcast.13, s32[16,32]{1,0:T(8,128)} %refs_3_.1), custom_call_target="tpu_custom_call" | custom-call | bytes 116736 | tf_op jit(solution)/shard_map/pallas_call | solution.py:38
  2.6 7.0 %all-to-all-start = ((f32[32,1,512]{2,1,0:T(1,128)}), f32[32,1,512]{2,1,0:T(1,128)S(1)}, u32[]{:S(2)}, u32[]{:S(2)}) async-start(f32[32,1,512]{2,1,0:T(1,128)} %bitcast.3), calls=%async_computation | async-start | bytes 131072 | tf_op jit(solution)/shard_map/all_to_all | solution.py:256
  9.6 0.3 %collective-permute-start.1 = (f32[3,2048]{1,0:T(4,128)S(1)}, f32[3,2048]{1,0:T(4,128)S(1)}, u32[]{:S(2)}, u32[]{:S(2)}) collective-permute-start(f32[3,2048]{1,0:T(4,128)S(1)} %get-tuple-element.7.refs_1_), channel_id=1, source_target_pairs={{0,1},{1,0},{2,3},{3,2},{4,5},{5,4},{6,7},{7,6},{8,9},{9,8},{10,11... | collective-permute-start | bytes 73736 | tf_op jit(solution)/shard_map/ppermute | solution.py:259
  9.9 1.0 %collective-permute-done.1.refs_3_ = f32[3,2048]{1,0:T(4,128)S(1)} collective-permute-done((f32[3,2048]{1,0:T(4,128)S(1)}, f32[3,2048]{1,0:T(4,128)S(1)}, u32[]{:S(2)}, u32[]{:S(2)}) %collective-permute-start.1) | collective-permute-done | bytes 24608 | tf_op jit(solution)/shard_map/ppermute | solution.py:259
  10.8 0.0 collective-permute-done.refs_2_
  10.9 2.5 %shard_map.69.refs_1_ = f32[16,128,128]{2,1,0:T(8,128)S(1)} custom-call(s32[2048,256]{1,0:T(8,128)} %refs_0_.1, f32[3,2048]{1,0:T(4,128)S(1)} %get-tuple-element.7.refs_1_, s32[2048,256]{1,0:T(8,128)S(1)} %collective-permute-done.refs_2_, f32[3,2048]{1,0:T(4,128)S(1)} %collective-permute-done.1.refs_3_), custom_call_target="tpu_custom_call" | custom-call | bytes 5292032 | tf_op jit(solution)/shard_map/pallas_call | solution.py:38
  13.4 3.6 %all-to-all-done = f32[32,1,512]{2,1,0:T(1,128)S(1)} async-done(((f32[32,1,512]{2,1,0:T(1,128)}), f32[32,1,512]{2,1,0:T(1,128)S(1)}, u32[]{:S(2)}, u32[]{:S(2)}) %all-to-all-start) | async-done | bytes 65568 | tf_op jit(solution)/shard_map/all_to_all | solution.py:256
  17.0 0.2 shard_map.70
  17.2 12.1 %all_to_all.10 = f32[32,1,2176]{2,1,0:T(1,128)S(1)} all-to-all(f32[32,1,2176]{2,1,0:T(1,128)S(1)} %bitcast.8), channel_id=1, replica_groups=mesh['far'=2,'near'=2,'line'=2,'chip'=2,'core'=2] {'core','near','line',..., dimensions={0} | all-to-all | bytes 557056 | tf_op jit(solution)/shard_map/all_to_all | solution.py:272
  29.3 0.1 shard_map.71.gain_ref
  29.4 0.3 %collective-permute-start.2 = (f32[8,256]{1,0:T(8,128)S(1)}, f32[8,256]{1,0:T(8,128)S(1)}, u32[]{:S(2)}, u32[]{:S(2)}) collective-permute-start(f32[8,256]{1,0:T(8,128)S(1)} %shard_map.71.gain_ref), channel_id=1, source_target_pairs={{0,1},{1,0},{2,3},{3,2},{4,5},{5,4},{6,7},{7,6},{8,9},{9,8},{10,11... | collective-permute-start | bytes 24584 | tf_op jit(solution)/shard_map/ppermute | solution.py:279
  29.7 0.9 %collective-permute-done.2.theirs_ref = f32[8,256]{1,0:T(8,128)S(1)} collective-permute-done((f32[8,256]{1,0:T(8,128)S(1)}, f32[8,256]{1,0:T(8,128)S(1)}, u32[]{:S(2)}, u32[]{:S(2)}) %collective-permute-start.2) | collective-permute-done | bytes 8224 | tf_op jit(solution)/shard_map/ppermute | solution.py:279
  30.6 0.7 %shard_map.72 = (f32[16,32]{1,0:T(8,128)}, f32[1,16]{1,0:T(1,128)}) custom-call(f32[8,256]{1,0:T(8,128)S(1)} %shard_map.71.gain_ref, f32[8,256]{1,0:T(8,128)S(1)} %collective-permute-done.2.theirs_ref), custom_call_target="tpu_custom_call" | custom-call | bytes 18496 | tf_op jit(solution)/shard_map/pallas_call | solution.py:38
Async XLA Ops:
  0.6 10.2 %collective-permute-start = (s32[2048,256]{1,0:T(8,128)}, s32[2048,256]{1,0:T(8,128)S(1)}, u32[]{:S(2)}, u32[]{:S(2)}) collective-permute-start(s32[2048,256]{1,0:T(8,128)} %refs_0_.1), channel_id=1, source_target_pairs={{0,1},{1,0},{2,3},{3,2},{4,5},{5,4},{6,7},{7,6},{8,9},{9,8},{10,11... | collective-permute-start | bytes 6291464 | tf_op jit(solution)/shard_map/ppermute | solution.py:240
  2.6 14.4 %all-to-all-start = ((f32[32,1,512]{2,1,0:T(1,128)}), f32[32,1,512]{2,1,0:T(1,128)S(1)}, u32[]{:S(2)}, u32[]{:S(2)}) async-start(f32[32,1,512]{2,1,0:T(1,128)} %bitcast.3), calls=%async_computation | async-start | bytes 131072 | tf_op jit(solution)/shard_map/all_to_all | solution.py:256
  9.6 1.3 %collective-permute-start.1 = (f32[3,2048]{1,0:T(4,128)S(1)}, f32[3,2048]{1,0:T(4,128)S(1)}, u32[]{:S(2)}, u32[]{:S(2)}) collective-permute-start(f32[3,2048]{1,0:T(4,128)S(1)} %get-tuple-element.7.refs_1_), channel_id=1, source_target_pairs={{0,1},{1,0},{2,3},{3,2},{4,5},{5,4},{6,7},{7,6},{8,9},{9,8},{10,11... | collective-permute-start | bytes 73736 | tf_op jit(solution)/shard_map/ppermute | solution.py:259
  29.4 1.2 %collective-permute-start.2 = (f32[8,256]{1,0:T(8,128)S(1)}, f32[8,256]{1,0:T(8,128)S(1)}, u32[]{:S(2)}, u32[]{:S(2)}) collective-permute-start(f32[8,256]{1,0:T(8,128)S(1)} %shard_map.71.gain_ref), channel_id=1, source_target_pairs={{0,1},{1,0},{2,3},{3,2},{4,5},{5,4},{6,7},{7,6},{8,9},{9,8},{10,11... | collective-permute-start | bytes 24584 | tf_op jit(solution)/shard_map/ppermute | solution.py:279

commit v5 on v4

--- a/solution.py
+++ b/solution.py
@@ -50,8 +50,12 @@
     return jax.ShapeDtypeStruct(shape, jnp.float32)
 
 
-def announce(groups, node_hbm, weight_hbm, label_hbm, split_hbm, out_ref, row_ref,
-             node_ref, weight_ref, label_ref, split_ref, block_ref, sems):
+def bf16(*shape):
+    return jax.ShapeDtypeStruct(shape, jnp.bfloat16)
+
+
+def announce(groups, bins_hbm, node_hbm, weight_hbm, label_hbm, split_hbm, out_ref, row_ref,
+             near_ref, node_ref, weight_ref, label_ref, split_ref, block_ref, sems):
     copies = [
         pltpu.make_async_copy(src, dst, sems.at[k])
         for k, (src, dst) in enumerate(
@@ -59,7 +63,18 @@
              (label_hbm, label_ref))
         )
     ]
-    for c in copies:
+    rows, half = near_ref.shape
+    part = rows // PARTS
+    first = pl.multiple_of(lax.axis_index("core") * half, half)
+    slabs = [
+        pltpu.make_async_copy(
+            bins_hbm.at[pl.ds(k * part, part), pl.ds(first, half)],
+            near_ref.at[pl.ds(k * part, part)],
+            sems.at[5 + k],
+        )
+        for k in range(PARTS)
+    ]
+    for c in copies + slabs:
         c.start()
     copies[0].wait()
     split = split_ref[...].astype(jnp.float32)
@@ -83,53 +98,41 @@
     row_ref[0:1] = node_ref[...].astype(jnp.float32)
     row_ref[1:2] = weight.astype(jnp.bfloat16).astype(jnp.float32)
     row_ref[2:3] = (weight * label_ref[...]).astype(jnp.bfloat16).astype(jnp.float32)
+    for c in slabs:
+        c.wait()
     out.wait()
 
 
-def histogram(nodes, bins_hbm, row_ref, far_bins, far_row, out_ref, bins_ref, sems):
-    rows, half = bins_ref.shape
-    part = rows // PARTS
-    first = pl.multiple_of(lax.axis_index("core") * half, half)
-    copies = [
-        pltpu.make_async_copy(
-            bins_hbm.at[pl.ds(k * part, part), pl.ds(first, half)],
-            bins_ref.at[pl.ds(k * part, part)],
-            sems.at[k],
-        )
-        for k in range(PARTS)
-    ]
-    for c in copies:
-        c.start()
-
-    def sides_of(ref):
-        node = ref[0:1].astype(jnp.int32)
-        hot = lax.broadcasted_iota(jnp.int32, (nodes, rows), 0) == node
-        return jnp.concatenate(
-            [jnp.where(hot, ref[1:2], 0.0), jnp.where(hot, ref[2:3], 0.0)], axis=0
-        ).astype(jnp.bfloat16)
-
-    def add(sides, bins, seed):
-        one, zero = jnp.bfloat16(1), jnp.bfloat16(0)
-        for b in range(0, BINS, 2):
-            acc = jnp.zeros((2 * nodes, 2 * half), jnp.float32)
-            for r in range(0, rows, STEP):
-                chunk = bins[r : r + STEP]
-                mask = jnp.concatenate(
-                    [jnp.where(chunk <= jnp.bfloat16(b + k), one, zero) for k in range(2)],
-                    axis=1,
-                )
-                acc += jnp.dot(
-                    sides[:, r : r + STEP], mask, preferred_element_type=jnp.float32
-                )
-            for k in range(2):
-                here = acc[:, k * half : (k + 1) * half]
-                out_ref[b + k] = here if seed else out_ref[b + k] + here
-
-    add(sides_of(far_row), far_bins[:, pl.ds(first, half)].astype(jnp.bfloat16), True)
-    sides = sides_of(row_ref)
-    for c in copies:
-        c.wait()
-    add(sides, bins_ref[...].astype(jnp.bfloat16), False)
+def sides_of(nodes, row_ref):
+    node = row_ref[0:1].astype(jnp.int32)
+    hot = lax.broadcasted_iota(jnp.int32, (nodes, node.shape[1]), 0) == node
+    return jnp.concatenate(
+        [jnp.where(hot, row_ref[1:2], 0.0), jnp.where(hot, row_ref[2:3], 0.0)], axis=0
+    ).astype(jnp.bfloat16)
+
+
+def histogram(nodes, bins_ref, row_ref, before_ref, out_ref):
+    half = out_ref.shape[2]
+    rows, width = bins_ref.shape
+    if width == half:
+        bins = bins_ref[...]
+    else:
+        first = pl.multiple_of(lax.axis_index("core") * half, half)
+        bins = bins_ref[:, pl.ds(first, half)]
+    bins = bins.astype(jnp.bfloat16)
+    sides = sides_of(nodes, row_ref)
+    one, zero = jnp.bfloat16(1), jnp.bfloat16(0)
+    for b in range(0, BINS, 2):
+        acc = jnp.zeros((2 * nodes, 2 * half), jnp.float32)
+        for r in range(0, rows, STEP):
+            chunk = bins[r : r + STEP]
+            mask = jnp.concatenate(
+                [jnp.where(chunk <= jnp.bfloat16(b + k), one, zero) for k in range(2)], axis=1
+            )
+            acc += jnp.dot(sides[:, r : r + STEP], mask, preferred_element_type=jnp.float32)
+        for k in range(2):
+            here = acc[:, k * half : (k + 1) * half]
+            out_ref[b + k] = here if before_ref is None else before_ref[b + k] + here
 
 
 def choose(sizes, groups, held, feat_part, half_n, got_ref, below_ref, out_ref):
@@ -241,16 +244,18 @@
     def k_announce(*refs):
         announce(groups, *refs)
     per_row = [x.reshape(1, rows_here) for x in (node_of, weight, label)]
-    block, row = call(
-        k_announce, [f32(n_all * held, LANES), f32(3, rows_here)], *per_row, split_bins,
-        place=[HBM] * 4, where=[HBM, VMEM],
+    block, row, near = call(
+        k_announce,
+        [f32(n_all * held, LANES), f32(3, rows_here),
+         jax.ShapeDtypeStruct((rows_here, half_f), jnp.int32)],
+        bins, *per_row, split_bins, place=[HBM] * 5, where=[HBM, VMEM, VMEM],
         scratch=[
             pltpu.VMEM((1, rows_here), jnp.int32),
             pltpu.VMEM((1, rows_here), jnp.float32),
             pltpu.VMEM((1, rows_here), jnp.float32),
             pltpu.VMEM(split_bins.shape, jnp.int32),
             pltpu.VMEM((n_all * held, LANES), jnp.float32),
-            pltpu.SemaphoreType.DMA((5,)),
+            pltpu.SemaphoreType.DMA((5 + PARTS,)),
         ],
     )
     got = lax.all_to_all(
@@ -258,13 +263,12 @@
     ).reshape(n_all * held, LANES)
     far_row = lax.ppermute(row, "core", pair)
 
-    def k_histogram(*refs):
+    def k_near(bins_ref, row_ref, out_ref):
+        histogram(nodes, bins_ref, row_ref, None, out_ref)
+    (below,) = call(k_near, [f32(BINS, 2 * nodes, half_f)], near, row)
+    def k_far(*refs):
         histogram(nodes, *refs)
-    (below,) = call(
-        k_histogram, [f32(BINS, 2 * nodes, half_f)], bins, row, far_bins, far_row,
-        place=[HBM, VMEM, VMEM, VMEM],
-        scratch=[pltpu.VMEM((rows_here, half_f), jnp.int32), pltpu.SemaphoreType.DMA((PARTS,))],
-    )
+    (below,) = call(k_far, [f32(BINS, 2 * nodes, half_f)], far_bins, far_row, below)
 
     def k_choose(*refs):
         choose(sizes, groups, held, feat_part, half_n, *refs)

time: 31.6 us -> 31.2 us (0.987)
  blocking collectives: 12.1 us -> 11.7 us
    ppermute x1, waiting for transfers between devices: 0.96 us -> 0.01 us  [shards(): far_row = lax.ppermute(row, 'core', pair)]
    all_to_all x1, waiting for transfers between devices: 3.6 us -> 4.51 us  [shards(): lax.all_to_all(block.reshape(n_all, 1, held * LANES), FIRST, 0, 0, tiled=...]
    all_to_all x1, blocking collectives: 12.1 us -> 11.7 us  [shards(): lax.all_to_all(parts.reshape(n_all, 1, lines * half_f), SECOND, 0, 0, til...]
    pallas_call x5 -> x6, Pallas kernels: 4.94 us -> 5 us  [call(): pl.pallas_call(kernel, out_shape=outs, in_specs=place, out_specs=tuple(wh...]
  transfers between devices with their start and end apart: 4 -> 4, of which waited for: 3 -> 2; matrix products, arithmetic and copies ran while one was open for 0% -> 0% of each run, Pallas kernels for 13% -> 13%
where the time goes in v5:
time: 31.2 us; the launch traced here: 31 us
  blocking collectives  11.7 us (38%)
  starting transfers between devices  8.11 us (26%)
  waiting for transfers between devices  5.44 us (17%)
  Pallas kernels  5 us (16%)
  between operations  0.7 us (2%)
    all_to_all x1, blocking collectives, shards(): lax.all_to_all(parts.reshape(n_all, 1, lines * half_f), SECOND, 0, 0, til...  11.7 us
    all_to_all x1, starting transfers between devices, shards(): lax.all_to_all(block.reshape(n_all, 1, held * LANES), FIRST, 0, 0, tiled=...  6.97 us
    pallas_call x6, Pallas kernels, call(): pl.pallas_call(kernel, out_shape=outs, in_specs=place, out_specs=tuple(wh...  5 us
    all_to_all x1, waiting for transfers between devices, shards(): lax.all_to_all(block.reshape(n_all, 1, held * LANES), FIRST, 0, 0, tiled=...  4.51 us
    ppermute x1, waiting for transfers between devices, shards(): other = lax.ppermute(gain, 'core', pair)  0.92 us
  transfers between devices with their start and end apart: 4, of which 2 were waited for; matrix products, arithmetic and copies ran while one was open for 0% of the time, Pallas kernels for 13%

profile of v5, /device:TPU:0, one launch (start us, length us, event | category | flops | bytes accessed | tf_op | source)
XLA Modules:
  0.0 31.0 jit_solution(3360821816959287085)
XLA Ops:
  0.6 0.5 %collective-permute-start = (s32[2048,256]{1,0:T(8,128)}, s32[2048,256]{1,0:T(8,128)S(1)}, u32[]{:S(2)}, u32[]{:S(2)}) collective-permute-start(s32[2048,256]{1,0:T(8,128)} %refs_0_.1), channel_id=1, source_target_pairs={{0,1},{1,0},{2,3},{3,2},{4,5},{5,4},{6,7},{7,6},{8,9},{9,8},{10,11... | collective-permute-start | bytes 6291464 | tf_op jit(solution)/shard_map/ppermute | solution.py:243
  1.1 1.5 %shard_map.68 = (f32[128,128]{1,0:T(8,128)}, f32[3,2048]{1,0:T(4,128)S(1)}, s32[2048,128]{1,0:T(8,128)S(1)}) custom-call(s32[2048,256]{1,0:T(8,128)} %refs_0_.1, s32[1,2048]{1,0:T(1,128)} %bitcast.11, f32[1,2048]{1,0:T(1,128)} %bitcast.12, f32[1,2048]{1,0:T(1,128)} %bitcast.13, s32[16,32]{1,0:T(8,128)} %refs_4_.1), custom_call_target="tpu_custom_call" | custom-call | bytes 3262464 | tf_op jit(solution)/shard_map/pallas_call | solution.py:38
  2.6 7.0 %all-to-all-start = ((f32[32,1,512]{2,1,0:T(1,128)}), f32[32,1,512]{2,1,0:T(1,128)S(1)}, u32[]{:S(2)}, u32[]{:S(2)}) async-start(f32[32,1,512]{2,1,0:T(1,128)} %bitcast.3), calls=%async_computation | async-start | bytes 131072 | tf_op jit(solution)/shard_map/all_to_all | solution.py:261
  9.6 0.3 %collective-permute-start.1 = (f32[3,2048]{1,0:T(4,128)S(1)}, f32[3,2048]{1,0:T(4,128)S(1)}, u32[]{:S(2)}, u32[]{:S(2)}) collective-permute-start(f32[3,2048]{1,0:T(4,128)S(1)} %get-tuple-element.8.row_ref), channel_id=1, source_target_pairs={{0,1},{1,0},{2,3},{3,2},{4,5},{5,4},{6,7},{7,6},{8,9},{9,8},{10,11... | collective-permute-start | bytes 73736 | tf_op jit(solution)/shard_map/ppermute | solution.py:264
  9.9 1.3 %shard_map.69.refs_2_ = f32[16,128,128]{2,1,0:T(8,128)S(1)} custom-call(s32[2048,128]{1,0:T(8,128)S(1)} %get-tuple-element.9.bins_ref, f32[3,2048]{1,0:T(4,128)S(1)} %get-tuple-element.8.row_ref), custom_call_target="tpu_custom_call" | custom-call | bytes 2121728 | tf_op jit(solution)/shard_map/pallas_call | solution.py:38
  11.2 0.0 collective-permute-done.1.refs_1_
  11.2 0.0 collective-permute-done.refs_0_
  11.2 1.3 %shard_map.70.refs_1_ = f32[16,128,128]{2,1,0:T(8,128)S(1)} custom-call(s32[2048,256]{1,0:T(8,128)S(1)} %collective-permute-done.refs_0_, f32[3,2048]{1,0:T(4,128)S(1)} %collective-permute-done.1.refs_1_, f32[16,128,128]{2,1,0:T(8,128)S(1)} %shard_map.69.refs_2_), custom_call_target="tpu_custom_call" | custom-call | bytes 4218880 | tf_op jit(solution)/shard_map/pallas_call | solution.py:38
  12.5 4.5 %all-to-all-done = f32[32,1,512]{2,1,0:T(1,128)S(1)} async-done(((f32[32,1,512]{2,1,0:T(1,128)}), f32[32,1,512]{2,1,0:T(1,128)S(1)}, u32[]{:S(2)}, u32[]{:S(2)}) %all-to-all-start) | async-done | bytes 65568 | tf_op jit(solution)/shard_map/all_to_all | solution.py:261
  17.0 0.2 shard_map.71
  17.2 11.7 %all_to_all.10 = f32[32,1,2176]{2,1,0:T(1,128)S(1)} all-to-all(f32[32,1,2176]{2,1,0:T(1,128)S(1)} %bitcast.8), channel_id=1, replica_groups=mesh['far'=2,'near'=2,'line'=2,'chip'=2,'core'=2] {'core','near','line',..., dimensions={0} | all-to-all | bytes 557056 | tf_op jit(solution)/shard_map/all_to_all | solution.py:276
  28.9 0.1 shard_map.72.gain_ref
  29.0 0.3 %collective-permute-start.2 = (f32[8,256]{1,0:T(8,128)S(1)}, f32[8,256]{1,0:T(8,128)S(1)}, u32[]{:S(2)}, u32[]{:S(2)}) collective-permute-start(f32[8,256]{1,0:T(8,128)S(1)} %shard_map.72.gain_ref), channel_id=1, source_target_pairs={{0,1},{1,0},{2,3},{3,2},{4,5},{5,4},{6,7},{7,6},{8,9},{9,8},{10,11... | collective-permute-start | bytes 24584 | tf_op jit(solution)/shard_map/ppermute | solution.py:283
  29.4 0.9 %collective-permute-done.2.theirs_ref = f32[8,256]{1,0:T(8,128)S(1)} collective-permute-done((f32[8,256]{1,0:T(8,128)S(1)}, f32[8,256]{1,0:T(8,128)S(1)}, u32[]{:S(2)}, u32[]{:S(2)}) %collective-permute-start.2) | collective-permute-done | bytes 8224 | tf_op jit(solution)/shard_map/ppermute | solution.py:283
  30.3 0.7 %shard_map.73 = (f32[16,32]{1,0:T(8,128)}, f32[1,16]{1,0:T(1,128)}) custom-call(f32[8,256]{1,0:T(8,128)S(1)} %shard_map.72.gain_ref, f32[8,256]{1,0:T(8,128)S(1)} %collective-permute-done.2.theirs_ref), custom_call_target="tpu_custom_call" | custom-call | bytes 18496 | tf_op jit(solution)/shard_map/pallas_call | solution.py:38
Async XLA Ops:
  0.6 10.6 %collective-permute-start = (s32[2048,256]{1,0:T(8,128)}, s32[2048,256]{1,0:T(8,128)S(1)}, u32[]{:S(2)}, u32[]{:S(2)}) collective-permute-start(s32[2048,256]{1,0:T(8,128)} %refs_0_.1), channel_id=1, source_target_pairs={{0,1},{1,0},{2,3},{3,2},{4,5},{5,4},{6,7},{7,6},{8,9},{9,8},{10,11... | collective-permute-start | bytes 6291464 | tf_op jit(solution)/shard_map/ppermute | solution.py:243
  2.6 14.4 %all-to-all-start = ((f32[32,1,512]{2,1,0:T(1,128)}), f32[32,1,512]{2,1,0:T(1,128)S(1)}, u32[]{:S(2)}, u32[]{:S(2)}) async-start(f32[32,1,512]{2,1,0:T(1,128)} %bitcast.3), calls=%async_computation | async-start | bytes 131072 | tf_op jit(solution)/shard_map/all_to_all | solution.py:261
  9.6 1.6 %collective-permute-start.1 = (f32[3,2048]{1,0:T(4,128)S(1)}, f32[3,2048]{1,0:T(4,128)S(1)}, u32[]{:S(2)}, u32[]{:S(2)}) collective-permute-start(f32[3,2048]{1,0:T(4,128)S(1)} %get-tuple-element.8.row_ref), channel_id=1, source_target_pairs={{0,1},{1,0},{2,3},{3,2},{4,5},{5,4},{6,7},{7,6},{8,9},{9,8},{10,11... | collective-permute-start | bytes 73736 | tf_op jit(solution)/shard_map/ppermute | solution.py:264
  29.0 1.2 %collective-permute-start.2 = (f32[8,256]{1,0:T(8,128)S(1)}, f32[8,256]{1,0:T(8,128)S(1)}, u32[]{:S(2)}, u32[]{:S(2)}) collective-permute-start(f32[8,256]{1,0:T(8,128)S(1)} %shard_map.72.gain_ref), channel_id=1, source_target_pairs={{0,1},{1,0},{2,3},{3,2},{4,5},{5,4},{6,7},{7,6},{8,9},{9,8},{10,11... | collective-permute-start | bytes 24584 | tf_op jit(solution)/shard_map/ppermute | solution.py:283

commit v6 on v5

--- a/solution.py
+++ b/solution.py
@@ -10,12 +10,12 @@
 ROWS = ("far", "near")
 FEAT = ("line", "chip", "core")
 ALL = ROWS + FEAT
-FIRST = ("far", "near", "line", "chip", "core")
+FIRST = ("core", "far", "near", "line", "chip")
 SECOND = ("core", "near", "line", "chip", "far")
 LANES = 128
 BINS = 16
-PARTS = 4
-STEP = 512
+PARTS = 1
+STEP = 2048
 VMEM = pl.BlockSpec(memory_space=pltpu.VMEM)
 HBM = pl.BlockSpec(memory_space=pltpu.HBM)
 ANY = pl.BlockSpec(memory_space=pl.ANY)

time: 31.2 us -> 31.1 us (level)
  no operation moved by 1% of the time
where the time goes in v6:
time: 31.1 us; the launch traced here: 30.9 us
  blocking collectives  11.7 us (38%)
  starting transfers between devices  8.11 us (26%)
  waiting for transfers between devices  5.35 us (17%)
  Pallas kernels  4.97 us (16%)
  between operations  0.7 us (2%)
    all_to_all x1, blocking collectives, shards(): lax.all_to_all(parts.reshape(n_all, 1, lines * half_f), SECOND, 0, 0, til...  11.7 us
    all_to_all x1, starting transfers between devices, shards(): lax.all_to_all(block.reshape(n_all, 1, held * LANES), FIRST, 0, 0, tiled=...  6.97 us
    pallas_call x6, Pallas kernels, call(): pl.pallas_call(kernel, out_shape=outs, in_specs=place, out_specs=tuple(wh...  4.97 us
    all_to_all x1, waiting for transfers between devices, shards(): lax.all_to_all(block.reshape(n_all, 1, held * LANES), FIRST, 0, 0, tiled=...  4.42 us
    ppermute x1, waiting for transfers between devices, shards(): other = lax.ppermute(gain, 'core', pair)  0.92 us
  transfers between devices with their start and end apart: 4, of which 2 were waited for; matrix products, arithmetic and copies ran while one was open for 0% of the time, Pallas kernels for 13%

profile of v6, /device:TPU:0, one launch (start us, length us, event | category | flops | bytes accessed | tf_op | source)
XLA Modules:
  0.0 30.9 jit_solution(1890715634669419818)
XLA Ops:
  0.6 0.5 %collective-permute-start = (s32[2048,256]{1,0:T(8,128)}, s32[2048,256]{1,0:T(8,128)S(1)}, u32[]{:S(2)}, u32[]{:S(2)}) collective-permute-start(s32[2048,256]{1,0:T(8,128)} %refs_0_.1), channel_id=1, source_target_pairs={{0,1},{1,0},{2,3},{3,2},{4,5},{5,4},{6,7},{7,6},{8,9},{9,8},{10,11... | collective-permute-start | bytes 6291464 | tf_op jit(solution)/shard_map/ppermute | solution.py:243
  1.1 1.5 %shard_map.68 = (f32[128,128]{1,0:T(8,128)}, f32[3,2048]{1,0:T(4,128)S(1)}, s32[2048,128]{1,0:T(8,128)S(1)}) custom-call(s32[2048,256]{1,0:T(8,128)} %refs_0_.1, s32[1,2048]{1,0:T(1,128)} %bitcast.11, f32[1,2048]{1,0:T(1,128)} %bitcast.12, f32[1,2048]{1,0:T(1,128)} %bitcast.13, s32[16,32]{1,0:T(8,128)} %refs_4_.1), custom_call_target="tpu_custom_call" | custom-call | bytes 3262464 | tf_op jit(solution)/shard_map/pallas_call | solution.py:38
  2.6 7.0 %all-to-all-start = ((f32[32,1,512]{2,1,0:T(1,128)}), f32[32,1,512]{2,1,0:T(1,128)S(1)}, u32[]{:S(2)}, u32[]{:S(2)}) async-start(f32[32,1,512]{2,1,0:T(1,128)} %bitcast.3), calls=%async_computation | async-start | bytes 131072 | tf_op jit(solution)/shard_map/all_to_all | solution.py:261
  9.6 0.3 %collective-permute-start.1 = (f32[3,2048]{1,0:T(4,128)S(1)}, f32[3,2048]{1,0:T(4,128)S(1)}, u32[]{:S(2)}, u32[]{:S(2)}) collective-permute-start(f32[3,2048]{1,0:T(4,128)S(1)} %get-tuple-element.8.row_ref), channel_id=1, source_target_pairs={{0,1},{1,0},{2,3},{3,2},{4,5},{5,4},{6,7},{7,6},{8,9},{9,8},{10,11... | collective-permute-start | bytes 73736 | tf_op jit(solution)/shard_map/ppermute | solution.py:264
  9.9 1.3 %shard_map.69.refs_2_ = f32[16,128,128]{2,1,0:T(8,128)S(1)} custom-call(s32[2048,128]{1,0:T(8,128)S(1)} %get-tuple-element.9.bins_ref, f32[3,2048]{1,0:T(4,128)S(1)} %get-tuple-element.8.row_ref), custom_call_target="tpu_custom_call" | custom-call | bytes 2121728 | tf_op jit(solution)/shard_map/pallas_call | solution.py:38
  11.2 0.0 collective-permute-done.1.refs_1_
  11.2 0.0 collective-permute-done.refs_0_
  11.2 1.3 %shard_map.70.refs_1_ = f32[16,128,128]{2,1,0:T(8,128)S(1)} custom-call(s32[2048,256]{1,0:T(8,128)S(1)} %collective-permute-done.refs_0_, f32[3,2048]{1,0:T(4,128)S(1)} %collective-permute-done.1.refs_1_, f32[16,128,128]{2,1,0:T(8,128)S(1)} %shard_map.69.refs_2_), custom_call_target="tpu_custom_call" | custom-call | bytes 4218880 | tf_op jit(solution)/shard_map/pallas_call | solution.py:38
  12.5 4.4 %all-to-all-done = f32[32,1,512]{2,1,0:T(1,128)S(1)} async-done(((f32[32,1,512]{2,1,0:T(1,128)}), f32[32,1,512]{2,1,0:T(1,128)S(1)}, u32[]{:S(2)}, u32[]{:S(2)}) %all-to-all-start) | async-done | bytes 65568 | tf_op jit(solution)/shard_map/all_to_all | solution.py:261
  16.9 0.2 shard_map.71
  17.1 11.7 %all_to_all.10 = f32[32,1,2176]{2,1,0:T(1,128)S(1)} all-to-all(f32[32,1,2176]{2,1,0:T(1,128)S(1)} %bitcast.8), channel_id=1, replica_groups=mesh['far'=2,'near'=2,'line'=2,'chip'=2,'core'=2] {'core','near','line',..., dimensions={0} | all-to-all | bytes 557056 | tf_op jit(solution)/shard_map/all_to_all | solution.py:276
  28.8 0.1 shard_map.72.gain_ref
  28.9 0.3 %collective-permute-start.2 = (f32[8,256]{1,0:T(8,128)S(1)}, f32[8,256]{1,0:T(8,128)S(1)}, u32[]{:S(2)}, u32[]{:S(2)}) collective-permute-start(f32[8,256]{1,0:T(8,128)S(1)} %shard_map.72.gain_ref), channel_id=1, source_target_pairs={{0,1},{1,0},{2,3},{3,2},{4,5},{5,4},{6,7},{7,6},{8,9},{9,8},{10,11... | collective-permute-start | bytes 24584 | tf_op jit(solution)/shard_map/ppermute | solution.py:283
  29.2 0.9 %collective-permute-done.2.theirs_ref = f32[8,256]{1,0:T(8,128)S(1)} collective-permute-done((f32[8,256]{1,0:T(8,128)S(1)}, f32[8,256]{1,0:T(8,128)S(1)}, u32[]{:S(2)}, u32[]{:S(2)}) %collective-permute-start.2) | collective-permute-done | bytes 8224 | tf_op jit(solution)/shard_map/ppermute | solution.py:283
  30.2 0.7 %shard_map.73 = (f32[16,32]{1,0:T(8,128)}, f32[1,16]{1,0:T(1,128)}) custom-call(f32[8,256]{1,0:T(8,128)S(1)} %shard_map.72.gain_ref, f32[8,256]{1,0:T(8,128)S(1)} %collective-permute-done.2.theirs_ref), custom_call_target="tpu_custom_call" | custom-call | bytes 18496 | tf_op jit(solution)/shard_map/pallas_call | solution.py:38
Async XLA Ops:
  0.6 10.5 %collective-permute-start = (s32[2048,256]{1,0:T(8,128)}, s32[2048,256]{1,0:T(8,128)S(1)}, u32[]{:S(2)}, u32[]{:S(2)}) collective-permute-start(s32[2048,256]{1,0:T(8,128)} %refs_0_.1), channel_id=1, source_target_pairs={{0,1},{1,0},{2,3},{3,2},{4,5},{5,4},{6,7},{7,6},{8,9},{9,8},{10,11... | collective-permute-start | bytes 6291464 | tf_op jit(solution)/shard_map/ppermute | solution.py:243
  2.6 14.3 %all-to-all-start = ((f32[32,1,512]{2,1,0:T(1,128)}), f32[32,1,512]{2,1,0:T(1,128)S(1)}, u32[]{:S(2)}, u32[]{:S(2)}) async-start(f32[32,1,512]{2,1,0:T(1,128)} %bitcast.3), calls=%async_computation | async-start | bytes 131072 | tf_op jit(solution)/shard_map/all_to_all | solution.py:261
  9.6 1.6 %collective-permute-start.1 = (f32[3,2048]{1,0:T(4,128)S(1)}, f32[3,2048]{1,0:T(4,128)S(1)}, u32[]{:S(2)}, u32[]{:S(2)}) collective-permute-start(f32[3,2048]{1,0:T(4,128)S(1)} %get-tuple-element.8.row_ref), channel_id=1, source_target_pairs={{0,1},{1,0},{2,3},{3,2},{4,5},{5,4},{6,7},{7,6},{8,9},{9,8},{10,11... | collective-permute-start | bytes 73736 | tf_op jit(solution)/shard_map/ppermute | solution.py:264
  28.9 1.2 %collective-permute-start.2 = (f32[8,256]{1,0:T(8,128)S(1)}, f32[8,256]{1,0:T(8,128)S(1)}, u32[]{:S(2)}, u32[]{:S(2)}) collective-permute-start(f32[8,256]{1,0:T(8,128)S(1)} %shard_map.72.gain_ref), channel_id=1, source_target_pairs={{0,1},{1,0},{2,3},{3,2},{4,5},{5,4},{6,7},{7,6},{8,9},{9,8},{10,11... | collective-permute-start | bytes 24584 | tf_op jit(solution)/shard_map/ppermute | solution.py:283

commit v7 on v6

--- a/solution.py
+++ b/solution.py
@@ -10,7 +10,7 @@
 ROWS = ("far", "near")
 FEAT = ("line", "chip", "core")
 ALL = ROWS + FEAT
-FIRST = ("core", "far", "near", "line", "chip")
+FIRST = ("near", "core", "far", "line", "chip")
 SECOND = ("core", "near", "line", "chip", "far")
 LANES = 128
 BINS = 16

time: 31.1 us -> 31 us (level)
  no operation moved by 1% of the time
where the time goes in v7:
time: 31 us; the launch traced here: 30.8 us
  blocking collectives  11.7 us (38%)
  starting transfers between devices  8.11 us (26%)
  waiting for transfers between devices  5.28 us (17%)
  Pallas kernels  4.97 us (16%)
  between operations  0.7 us (2%)
    all_to_all x1, blocking collectives, shards(): lax.all_to_all(parts.reshape(n_all, 1, lines * half_f), SECOND, 0, 0, til...  11.7 us
    all_to_all x1, starting transfers between devices, shards(): lax.all_to_all(block.reshape(n_all, 1, held * LANES), FIRST, 0, 0, tiled=...  6.97 us
    pallas_call x6, Pallas kernels, call(): pl.pallas_call(kernel, out_shape=outs, in_specs=place, out_specs=tuple(wh...  4.97 us
    all_to_all x1, waiting for transfers between devices, shards(): lax.all_to_all(block.reshape(n_all, 1, held * LANES), FIRST, 0, 0, tiled=...  4.36 us
    ppermute x1, waiting for transfers between devices, shards(): other = lax.ppermute(gain, 'core', pair)  0.92 us
  transfers between devices with their start and end apart: 4, of which 2 were waited for; matrix products, arithmetic and copies ran while one was open for 0% of the time, Pallas kernels for 13%

profile of v7, /device:TPU:0, one launch (start us, length us, event | category | flops | bytes accessed | tf_op | source)
XLA Modules:
  0.0 30.8 jit_solution(3134817082765994673)
XLA Ops:
  0.6 0.5 %collective-permute-start = (s32[2048,256]{1,0:T(8,128)}, s32[2048,256]{1,0:T(8,128)S(1)}, u32[]{:S(2)}, u32[]{:S(2)}) collective-permute-start(s32[2048,256]{1,0:T(8,128)} %refs_0_.1), channel_id=1, source_target_pairs={{0,1},{1,0},{2,3},{3,2},{4,5},{5,4},{6,7},{7,6},{8,9},{9,8},{10,11... | collective-permute-start | bytes 6291464 | tf_op jit(solution)/shard_map/ppermute | solution.py:243
  1.1 1.5 %shard_map.68 = (f32[128,128]{1,0:T(8,128)}, f32[3,2048]{1,0:T(4,128)S(1)}, s32[2048,128]{1,0:T(8,128)S(1)}) custom-call(s32[2048,256]{1,0:T(8,128)} %refs_0_.1, s32[1,2048]{1,0:T(1,128)} %bitcast.11, f32[1,2048]{1,0:T(1,128)} %bitcast.12, f32[1,2048]{1,0:T(1,128)} %bitcast.13, s32[16,32]{1,0:T(8,128)} %refs_4_.1), custom_call_target="tpu_custom_call" | custom-call | bytes 3262464 | tf_op jit(solution)/shard_map/pallas_call | solution.py:38
  2.6 7.0 %all-to-all-start = ((f32[32,1,512]{2,1,0:T(1,128)}), f32[32,1,512]{2,1,0:T(1,128)S(1)}, u32[]{:S(2)}, u32[]{:S(2)}) async-start(f32[32,1,512]{2,1,0:T(1,128)} %bitcast.3), calls=%async_computation | async-start | bytes 131072 | tf_op jit(solution)/shard_map/all_to_all | solution.py:261
  9.6 0.3 %collective-permute-start.1 = (f32[3,2048]{1,0:T(4,128)S(1)}, f32[3,2048]{1,0:T(4,128)S(1)}, u32[]{:S(2)}, u32[]{:S(2)}) collective-permute-start(f32[3,2048]{1,0:T(4,128)S(1)} %get-tuple-element.8.row_ref), channel_id=1, source_target_pairs={{0,1},{1,0},{2,3},{3,2},{4,5},{5,4},{6,7},{7,6},{8,9},{9,8},{10,11... | collective-permute-start | bytes 73736 | tf_op jit(solution)/shard_map/ppermute | solution.py:264
  9.9 1.3 %shard_map.69.refs_2_ = f32[16,128,128]{2,1,0:T(8,128)S(1)} custom-call(s32[2048,128]{1,0:T(8,128)S(1)} %get-tuple-element.9.bins_ref, f32[3,2048]{1,0:T(4,128)S(1)} %get-tuple-element.8.row_ref), custom_call_target="tpu_custom_call" | custom-call | bytes 2121728 | tf_op jit(solution)/shard_map/pallas_call | solution.py:38
  11.2 0.0 collective-permute-done.1.refs_1_
  11.2 0.0 collective-permute-done.refs_0_
  11.2 1.3 %shard_map.70.refs_1_ = f32[16,128,128]{2,1,0:T(8,128)S(1)} custom-call(s32[2048,256]{1,0:T(8,128)S(1)} %collective-permute-done.refs_0_, f32[3,2048]{1,0:T(4,128)S(1)} %collective-permute-done.1.refs_1_, f32[16,128,128]{2,1,0:T(8,128)S(1)} %shard_map.69.refs_2_), custom_call_target="tpu_custom_call" | custom-call | bytes 4218880 | tf_op jit(solution)/shard_map/pallas_call | solution.py:38
  12.5 4.4 %all-to-all-done = f32[32,1,512]{2,1,0:T(1,128)S(1)} async-done(((f32[32,1,512]{2,1,0:T(1,128)}), f32[32,1,512]{2,1,0:T(1,128)S(1)}, u32[]{:S(2)}, u32[]{:S(2)}) %all-to-all-start) | async-done | bytes 65568 | tf_op jit(solution)/shard_map/all_to_all | solution.py:261
  16.8 0.2 shard_map.71
  17.0 11.7 %all_to_all.10 = f32[32,1,2176]{2,1,0:T(1,128)S(1)} all-to-all(f32[32,1,2176]{2,1,0:T(1,128)S(1)} %bitcast.8), channel_id=1, replica_groups=mesh['far'=2,'near'=2,'line'=2,'chip'=2,'core'=2] {'core','near','line',..., dimensions={0} | all-to-all | bytes 557056 | tf_op jit(solution)/shard_map/all_to_all | solution.py:276
  28.8 0.1 shard_map.72.gain_ref
  28.9 0.3 %collective-permute-start.2 = (f32[8,256]{1,0:T(8,128)S(1)}, f32[8,256]{1,0:T(8,128)S(1)}, u32[]{:S(2)}, u32[]{:S(2)}) collective-permute-start(f32[8,256]{1,0:T(8,128)S(1)} %shard_map.72.gain_ref), channel_id=1, source_target_pairs={{0,1},{1,0},{2,3},{3,2},{4,5},{5,4},{6,7},{7,6},{8,9},{9,8},{10,11... | collective-permute-start | bytes 24584 | tf_op jit(solution)/shard_map/ppermute | solution.py:283
  29.2 0.9 %collective-permute-done.2.theirs_ref = f32[8,256]{1,0:T(8,128)S(1)} collective-permute-done((f32[8,256]{1,0:T(8,128)S(1)}, f32[8,256]{1,0:T(8,128)S(1)}, u32[]{:S(2)}, u32[]{:S(2)}) %collective-permute-start.2) | collective-permute-done | bytes 8224 | tf_op jit(solution)/shard_map/ppermute | solution.py:283
  30.1 0.7 %shard_map.73 = (f32[16,32]{1,0:T(8,128)}, f32[1,16]{1,0:T(1,128)}) custom-call(f32[8,256]{1,0:T(8,128)S(1)} %shard_map.72.gain_ref, f32[8,256]{1,0:T(8,128)S(1)} %collective-permute-done.2.theirs_ref), custom_call_target="tpu_custom_call" | custom-call | bytes 18496 | tf_op jit(solution)/shard_map/pallas_call | solution.py:38
Async XLA Ops:
  0.6 10.5 %collective-permute-start = (s32[2048,256]{1,0:T(8,128)}, s32[2048,256]{1,0:T(8,128)S(1)}, u32[]{:S(2)}, u32[]{:S(2)}) collective-permute-start(s32[2048,256]{1,0:T(8,128)} %refs_0_.1), channel_id=1, source_target_pairs={{0,1},{1,0},{2,3},{3,2},{4,5},{5,4},{6,7},{7,6},{8,9},{9,8},{10,11... | collective-permute-start | bytes 6291464 | tf_op jit(solution)/shard_map/ppermute | solution.py:243
  2.6 14.2 %all-to-all-start = ((f32[32,1,512]{2,1,0:T(1,128)}), f32[32,1,512]{2,1,0:T(1,128)S(1)}, u32[]{:S(2)}, u32[]{:S(2)}) async-start(f32[32,1,512]{2,1,0:T(1,128)} %bitcast.3), calls=%async_computation | async-start | bytes 131072 | tf_op jit(solution)/shard_map/all_to_all | solution.py:261
  9.6 1.6 %collective-permute-start.1 = (f32[3,2048]{1,0:T(4,128)S(1)}, f32[3,2048]{1,0:T(4,128)S(1)}, u32[]{:S(2)}, u32[]{:S(2)}) collective-permute-start(f32[3,2048]{1,0:T(4,128)S(1)} %get-tuple-element.8.row_ref), channel_id=1, source_target_pairs={{0,1},{1,0},{2,3},{3,2},{4,5},{5,4},{6,7},{7,6},{8,9},{9,8},{10,11... | collective-permute-start | bytes 73736 | tf_op jit(solution)/shard_map/ppermute | solution.py:264
  28.9 1.2 %collective-permute-start.2 = (f32[8,256]{1,0:T(8,128)S(1)}, f32[8,256]{1,0:T(8,128)S(1)}, u32[]{:S(2)}, u32[]{:S(2)}) collective-permute-start(f32[8,256]{1,0:T(8,128)S(1)} %shard_map.72.gain_ref), channel_id=1, source_target_pairs={{0,1},{1,0},{2,3},{3,2},{4,5},{5,4},{6,7},{7,6},{8,9},{9,8},{10,11... | collective-permute-start | bytes 24584 | tf_op jit(solution)/shard_map/ppermute | solution.py:283

commit v8 on v7

--- a/solution.py
+++ b/solution.py
@@ -211,20 +211,26 @@
     ) / (total0 + 1.0)
 
 
-def finish(gain_ref, theirs_ref, out_ref, best_ref):
+def finish(gain_ref, theirs_ref, out_hbm, best_hbm, out_ref, best_ref, sems):
     mine, theirs = gain_ref[...], theirs_ref[...]
     first = lax.axis_index("core") == 0
     gain = jnp.concatenate(
         [jnp.where(first, mine, theirs), jnp.where(first, theirs, mine)], axis=0
     )
+    feats, width = gain.shape[1], out_ref.shape[1]
+    own = lax.axis_index(FEAT) * width
+    turned = pltpu.roll(gain, lax.rem(feats - own, feats), 1)
+    out_ref[...] = turned[:, : out_ref.shape[1]]
+    gain_out = pltpu.make_async_copy(out_ref, out_hbm, sems.at[0])
+    gain_out.start()
     n = gain.shape[0]
     best = jnp.max(gain, axis=1, keepdims=True)
     eye = lax.broadcasted_iota(jnp.int32, (n, n), 0) == lax.broadcasted_iota(jnp.int32, (n, n), 1)
     best_ref[...] = jnp.sum(jnp.where(eye, best, 0.0), axis=0, keepdims=True)
-    feats, width = gain.shape[1], out_ref.shape[1]
-    own = lax.axis_index(FEAT) * width
-    turned = pltpu.roll(gain, lax.rem(feats - own, feats), 1)
-    out_ref[...] = turned[:, : out_ref.shape[1]]
+    best_out = pltpu.make_async_copy(best_ref, best_hbm, sems.at[1])
+    best_out.start()
+    gain_out.wait()
+    best_out.wait()
 
 
 def shards(bins, node_of, weight, label, split_bins):
@@ -282,7 +288,13 @@
     (gain,) = call(k_gain, [f32(half_n, feats)], parts)
     other = lax.ppermute(gain, "core", pair)
     out, best = call(
-        finish, [f32(node_part, feat_part), f32(1, node_part)], gain, other
+        finish, [f32(node_part, feat_part), f32(1, node_part)], gain, other,
+        where=[HBM, HBM],
+        scratch=[
+            pltpu.VMEM((node_part, feat_part), jnp.float32),
+            pltpu.VMEM((1, node_part), jnp.float32),
+            pltpu.SemaphoreType.DMA((2,)),
+        ],
     )
     return out, best.reshape(node_part)
 

time: 31 us -> 31.1 us (level)
  no operation moved by 1% of the time
where the time goes in v8:
time: 31.1 us; the launch traced here: 30.8 us
  blocking collectives  11.7 us (38%)
  starting transfers between devices  8.11 us (26%)
  waiting for transfers between devices  5.28 us (17%)
  Pallas kernels  4.99 us (16%)
  between operations  0.7 us (2%)
    all_to_all x1, blocking collectives, shards(): lax.all_to_all(parts.reshape(n_all, 1, lines * half_f), SECOND, 0, 0, til...  11.7 us
    all_to_all x1, starting transfers between devices, shards(): lax.all_to_all(block.reshape(n_all, 1, held * LANES), FIRST, 0, 0, tiled=...  6.97 us
    pallas_call x6, Pallas kernels, call(): pl.pallas_call(kernel, out_shape=outs, in_specs=place, out_specs=tuple(wh...  4.99 us
    all_to_all x1, waiting for transfers between devices, shards(): lax.all_to_all(block.reshape(n_all, 1, held * LANES), FIRST, 0, 0, tiled=...  4.36 us
    ppermute x1, waiting for transfers between devices, shards(): other = lax.ppermute(gain, 'core', pair)  0.92 us
  transfers between devices with their start and end apart: 4, of which 2 were waited for; matrix products, arithmetic and copies ran while one was open for 0% of the time, Pallas kernels for 13%

profile of v8, /device:TPU:0, one launch (start us, length us, event | category | flops | bytes accessed | tf_op | source)
XLA Modules:
  0.0 30.8 jit_solution(15047898938564152521)
XLA Ops:
  0.6 0.5 %collective-permute-start = (s32[2048,256]{1,0:T(8,128)}, s32[2048,256]{1,0:T(8,128)S(1)}, u32[]{:S(2)}, u32[]{:S(2)}) collective-permute-start(s32[2048,256]{1,0:T(8,128)} %refs_0_.1), channel_id=1, source_target_pairs={{0,1},{1,0},{2,3},{3,2},{4,5},{5,4},{6,7},{7,6},{8,9},{9,8},{10,11... | collective-permute-start | bytes 6291464 | tf_op jit(solution)/shard_map/ppermute | solution.py:249
  1.1 1.5 %shard_map.68 = (f32[128,128]{1,0:T(8,128)}, f32[3,2048]{1,0:T(4,128)S(1)}, s32[2048,128]{1,0:T(8,128)S(1)}) custom-call(s32[2048,256]{1,0:T(8,128)} %refs_0_.1, s32[1,2048]{1,0:T(1,128)} %bitcast.11, f32[1,2048]{1,0:T(1,128)} %bitcast.12, f32[1,2048]{1,0:T(1,128)} %bitcast.13, s32[16,32]{1,0:T(8,128)} %refs_4_.1), custom_call_target="tpu_custom_call" | custom-call | bytes 3262464 | tf_op jit(solution)/shard_map/pallas_call | solution.py:38
  2.6 7.0 %all-to-all-start = ((f32[32,1,512]{2,1,0:T(1,128)}), f32[32,1,512]{2,1,0:T(1,128)S(1)}, u32[]{:S(2)}, u32[]{:S(2)}) async-start(f32[32,1,512]{2,1,0:T(1,128)} %bitcast.3), calls=%async_computation | async-start | bytes 131072 | tf_op jit(solution)/shard_map/all_to_all | solution.py:267
  9.6 0.3 %collective-permute-start.1 = (f32[3,2048]{1,0:T(4,128)S(1)}, f32[3,2048]{1,0:T(4,128)S(1)}, u32[]{:S(2)}, u32[]{:S(2)}) collective-permute-start(f32[3,2048]{1,0:T(4,128)S(1)} %get-tuple-element.8.row_ref), channel_id=1, source_target_pairs={{0,1},{1,0},{2,3},{3,2},{4,5},{5,4},{6,7},{7,6},{8,9},{9,8},{10,11... | collective-permute-start | bytes 73736 | tf_op jit(solution)/shard_map/ppermute | solution.py:270
  9.9 1.3 %shard_map.69.refs_2_ = f32[16,128,128]{2,1,0:T(8,128)S(1)} custom-call(s32[2048,128]{1,0:T(8,128)S(1)} %get-tuple-element.9.bins_ref, f32[3,2048]{1,0:T(4,128)S(1)} %get-tuple-element.8.row_ref), custom_call_target="tpu_custom_call" | custom-call | bytes 2121728 | tf_op jit(solution)/shard_map/pallas_call | solution.py:38
  11.2 0.0 collective-permute-done.1.refs_1_
  11.2 0.0 collective-permute-done.refs_0_
  11.2 1.3 %shard_map.70.refs_1_ = f32[16,128,128]{2,1,0:T(8,128)S(1)} custom-call(s32[2048,256]{1,0:T(8,128)S(1)} %collective-permute-done.refs_0_, f32[3,2048]{1,0:T(4,128)S(1)} %collective-permute-done.1.refs_1_, f32[16,128,128]{2,1,0:T(8,128)S(1)} %shard_map.69.refs_2_), custom_call_target="tpu_custom_call" | custom-call | bytes 4218880 | tf_op jit(solution)/shard_map/pallas_call | solution.py:38
  12.5 4.4 %all-to-all-done = f32[32,1,512]{2,1,0:T(1,128)S(1)} async-done(((f32[32,1,512]{2,1,0:T(1,128)}), f32[32,1,512]{2,1,0:T(1,128)S(1)}, u32[]{:S(2)}, u32[]{:S(2)}) %all-to-all-start) | async-done | bytes 65568 | tf_op jit(solution)/shard_map/all_to_all | solution.py:267
  16.8 0.2 shard_map.71
  17.0 11.7 %all_to_all.10 = f32[32,1,2176]{2,1,0:T(1,128)S(1)} all-to-all(f32[32,1,2176]{2,1,0:T(1,128)S(1)} %bitcast.8), channel_id=1, replica_groups=mesh['far'=2,'near'=2,'line'=2,'chip'=2,'core'=2] {'core','near','line',..., dimensions={0} | all-to-all | bytes 557056 | tf_op jit(solution)/shard_map/all_to_all | solution.py:282
  28.8 0.1 shard_map.72.gain_ref
  28.9 0.3 %collective-permute-start.2 = (f32[8,256]{1,0:T(8,128)S(1)}, f32[8,256]{1,0:T(8,128)S(1)}, u32[]{:S(2)}, u32[]{:S(2)}) collective-permute-start(f32[8,256]{1,0:T(8,128)S(1)} %shard_map.72.gain_ref), channel_id=1, source_target_pairs={{0,1},{1,0},{2,3},{3,2},{4,5},{5,4},{6,7},{7,6},{8,9},{9,8},{10,11... | collective-permute-start | bytes 24584 | tf_op jit(solution)/shard_map/ppermute | solution.py:289
  29.2 0.9 %collective-permute-done.2.theirs_ref = f32[8,256]{1,0:T(8,128)S(1)} collective-permute-done((f32[8,256]{1,0:T(8,128)S(1)}, f32[8,256]{1,0:T(8,128)S(1)}, u32[]{:S(2)}, u32[]{:S(2)}) %collective-permute-start.2) | collective-permute-done | bytes 8224 | tf_op jit(solution)/shard_map/ppermute | solution.py:289
  30.1 0.7 %shard_map.73 = (f32[16,32]{1,0:T(8,128)}, f32[1,16]{1,0:T(1,128)}) custom-call(f32[8,256]{1,0:T(8,128)S(1)} %shard_map.72.gain_ref, f32[8,256]{1,0:T(8,128)S(1)} %collective-permute-done.2.theirs_ref), custom_call_target="tpu_custom_call" | custom-call | bytes 18496 | tf_op jit(solution)/shard_map/pallas_call | solution.py:38
Async XLA Ops:
  0.6 10.5 %collective-permute-start = (s32[2048,256]{1,0:T(8,128)}, s32[2048,256]{1,0:T(8,128)S(1)}, u32[]{:S(2)}, u32[]{:S(2)}) collective-permute-start(s32[2048,256]{1,0:T(8,128)} %refs_0_.1), channel_id=1, source_target_pairs={{0,1},{1,0},{2,3},{3,2},{4,5},{5,4},{6,7},{7,6},{8,9},{9,8},{10,11... | collective-permute-start | bytes 6291464 | tf_op jit(solution)/shard_map/ppermute | solution.py:249
  2.6 14.2 %all-to-all-start = ((f32[32,1,512]{2,1,0:T(1,128)}), f32[32,1,512]{2,1,0:T(1,128)S(1)}, u32[]{:S(2)}, u32[]{:S(2)}) async-start(f32[32,1,512]{2,1,0:T(1,128)} %bitcast.3), calls=%async_computation | async-start | bytes 131072 | tf_op jit(solution)/shard_map/all_to_all | solution.py:267
  9.6 1.6 %collective-permute-start.1 = (f32[3,2048]{1,0:T(4,128)S(1)}, f32[3,2048]{1,0:T(4,128)S(1)}, u32[]{:S(2)}, u32[]{:S(2)}) collective-permute-start(f32[3,2048]{1,0:T(4,128)S(1)} %get-tuple-element.8.row_ref), channel_id=1, source_target_pairs={{0,1},{1,0},{2,3},{3,2},{4,5},{5,4},{6,7},{7,6},{8,9},{9,8},{10,11... | collective-permute-start | bytes 73736 | tf_op jit(solution)/shard_map/ppermute | solution.py:270
  28.9 1.2 %collective-permute-start.2 = (f32[8,256]{1,0:T(8,128)S(1)}, f32[8,256]{1,0:T(8,128)S(1)}, u32[]{:S(2)}, u32[]{:S(2)}) collective-permute-start(f32[8,256]{1,0:T(8,128)S(1)} %shard_map.72.gain_ref), channel_id=1, source_target_pairs={{0,1},{1,0},{2,3},{3,2},{4,5},{5,4},{6,7},{7,6},{8,9},{9,8},{10,11... | collective-permute-start | bytes 24584 | tf_op jit(solution)/shard_map/ppermute | solution.py:289

commit v9 on v7

--- a/solution.py
+++ b/solution.py
@@ -135,7 +135,7 @@
             out_ref[b + k] = here if before_ref is None else before_ref[b + k] + here
 
 
-def choose(sizes, groups, held, feat_part, half_n, got_ref, below_ref, out_ref):
+def choose(sizes, groups, held, feat_part, half_n, got_ref, below_ref, total_ref, out_ref):
     half = below_ref.shape[2]
     nodes = below_ref.shape[1] // 2
     mine = half // feat_part
@@ -162,11 +162,7 @@
         further = split >= b
         left0 = jnp.where(further, below_ref[b, :nodes], left0)
         left1 = jnp.where(further, below_ref[b, nodes:], left1)
-    everything = below_ref[BINS - 1]
-    eye = lax.broadcasted_iota(jnp.int32, everything.shape, 0) == lax.broadcasted_iota(
-        jnp.int32, everything.shape, 1
-    )
-    total = jnp.sum(jnp.where(eye, everything, 0.0), axis=0, keepdims=True)
+    total = total_ref[...]
     lines = 2 * half_n + 1
     for z in range(n_rows):
         for c in range(2):
@@ -266,13 +262,20 @@
     def k_near(bins_ref, row_ref, out_ref):
         histogram(nodes, bins_ref, row_ref, None, out_ref)
     (below,) = call(k_near, [f32(BINS, 2 * nodes, half_f)], near, row)
-    def k_far(*refs):
-        histogram(nodes, *refs)
-    (below,) = call(k_far, [f32(BINS, 2 * nodes, half_f)], far_bins, far_row, below)
+    def k_far(bins_ref, row_ref, before_ref, out_ref, total_ref):
+        histogram(nodes, bins_ref, row_ref, before_ref, out_ref)
+        everything = out_ref[BINS - 1]
+        eye = lax.broadcasted_iota(jnp.int32, everything.shape, 0) == lax.broadcasted_iota(
+            jnp.int32, everything.shape, 1
+        )
+        total_ref[...] = jnp.sum(jnp.where(eye, everything, 0.0), axis=0, keepdims=True)
+    below, total = call(
+        k_far, [f32(BINS, 2 * nodes, half_f), f32(1, 2 * nodes)], far_bins, far_row, below
+    )
 
     def k_choose(*refs):
         choose(sizes, groups, held, feat_part, half_n, *refs)
-    (parts,) = call(k_choose, [f32(n_all * lines, half_f)], got, below)
+    (parts,) = call(k_choose, [f32(n_all * lines, half_f)], got, below, total)
     parts = lax.all_to_all(
         parts.reshape(n_all, 1, lines * half_f), SECOND, 0, 0, tiled=True
     ).reshape(n_all * lines, half_f)

time: 31 us -> 31 us (level)
  no operation moved by 1% of the time
where the time goes in v9:
time: 31 us; the launch traced here: 30.8 us
  blocking collectives  11.7 us (38%)
  starting transfers between devices  8.11 us (26%)
  waiting for transfers between devices  5.28 us (17%)
  Pallas kernels  4.98 us (16%)
  between operations  0.69 us (2%)
    all_to_all x1, blocking collectives, shards(): lax.all_to_all(parts.reshape(n_all, 1, lines * half_f), SECOND, 0, 0, til...  11.7 us
    all_to_all x1, starting transfers between devices, shards(): lax.all_to_all(block.reshape(n_all, 1, held * LANES), FIRST, 0, 0, tiled=...  6.97 us
    pallas_call x6, Pallas kernels, call(): pl.pallas_call(kernel, out_shape=outs, in_specs=place, out_specs=tuple(wh...  4.98 us
    all_to_all x1, waiting for transfers between devices, shards(): lax.all_to_all(block.reshape(n_all, 1, held * LANES), FIRST, 0, 0, tiled=...  4.35 us
    ppermute x1, waiting for transfers between devices, shards(): other = lax.ppermute(gain, 'core', pair)  0.92 us
  transfers between devices with their start and end apart: 4, of which 2 were waited for; matrix products, arithmetic and copies ran while one was open for 0% of the time, Pallas kernels for 13%

profile of v9, /device:TPU:0, one launch (start us, length us, event | category | flops | bytes accessed | tf_op | source)
XLA Modules:
  0.0 30.8 jit_solution(14976719734047310726)
XLA Ops:
  0.6 0.5 %collective-permute-start = (s32[2048,256]{1,0:T(8,128)}, s32[2048,256]{1,0:T(8,128)S(1)}, u32[]{:S(2)}, u32[]{:S(2)}) collective-permute-start(s32[2048,256]{1,0:T(8,128)} %refs_0_.1), channel_id=1, source_target_pairs={{0,1},{1,0},{2,3},{3,2},{4,5},{5,4},{6,7},{7,6},{8,9},{9,8},{10,11... | collective-permute-start | bytes 6291464 | tf_op jit(solution)/shard_map/ppermute | solution.py:239
  1.1 1.4 %shard_map.68 = (f32[128,128]{1,0:T(8,128)}, f32[3,2048]{1,0:T(4,128)S(1)}, s32[2048,128]{1,0:T(8,128)S(1)}) custom-call(s32[2048,256]{1,0:T(8,128)} %refs_0_.1, s32[1,2048]{1,0:T(1,128)} %bitcast.11, f32[1,2048]{1,0:T(1,128)} %bitcast.12, f32[1,2048]{1,0:T(1,128)} %bitcast.13, s32[16,32]{1,0:T(8,128)} %refs_4_.1), custom_call_target="tpu_custom_call" | custom-call | bytes 3262464 | tf_op jit(solution)/shard_map/pallas_call | solution.py:38
  2.6 7.0 %all-to-all-start = ((f32[32,1,512]{2,1,0:T(1,128)}), f32[32,1,512]{2,1,0:T(1,128)S(1)}, u32[]{:S(2)}, u32[]{:S(2)}) async-start(f32[32,1,512]{2,1,0:T(1,128)} %bitcast.3), calls=%async_computation | async-start | bytes 131072 | tf_op jit(solution)/shard_map/all_to_all | solution.py:257
  9.6 0.3 %collective-permute-start.1 = (f32[3,2048]{1,0:T(4,128)S(1)}, f32[3,2048]{1,0:T(4,128)S(1)}, u32[]{:S(2)}, u32[]{:S(2)}) collective-permute-start(f32[3,2048]{1,0:T(4,128)S(1)} %get-tuple-element.10.row_ref), channel_id=1, source_target_pairs={{0,1},{1,0},{2,3},{3,2},{4,5},{5,4},{6,7},{7,6},{8,9},{9,8},{10,11... | collective-permute-start | bytes 73736 | tf_op jit(solution)/shard_map/ppermute | solution.py:260
  9.9 1.3 %shard_map.69.before_ref = f32[16,128,128]{2,1,0:T(8,128)S(1)} custom-call(s32[2048,128]{1,0:T(8,128)S(1)} %get-tuple-element.11.bins_ref, f32[3,2048]{1,0:T(4,128)S(1)} %get-tuple-element.10.row_ref), custom_call_target="tpu_custom_call" | custom-call | bytes 2121728 | tf_op jit(solution)/shard_map/pallas_call | solution.py:38
  11.2 0.0 collective-permute-done.1.row_ref
  11.2 0.0 collective-permute-done.bins_ref
  11.2 1.3 %shard_map.70 = (f32[16,128,128]{2,1,0:T(8,128)S(1)}, f32[1,128]{1,0:T(1,128)S(1)}) custom-call(s32[2048,256]{1,0:T(8,128)S(1)} %collective-permute-done.bins_ref, f32[3,2048]{1,0:T(4,128)S(1)} %collective-permute-done.1.row_ref, f32[16,128,128]{2,1,0:T(8,128)S(1)} %shard_map.69.before_ref), custom_call_target="tpu_custom_call" | custom-call | bytes 4219392 | tf_op jit(solution)/shard_map/pallas_call | solution.py:38
  12.5 4.3 %all-to-all-done = f32[32,1,512]{2,1,0:T(1,128)S(1)} async-done(((f32[32,1,512]{2,1,0:T(1,128)}), f32[32,1,512]{2,1,0:T(1,128)S(1)}, u32[]{:S(2)}, u32[]{:S(2)}) %all-to-all-start) | async-done | bytes 65568 | tf_op jit(solution)/shard_map/all_to_all | solution.py:257
  16.8 0.2 shard_map.71
  17.0 11.7 %all_to_all.10 = f32[32,1,2176]{2,1,0:T(1,128)S(1)} all-to-all(f32[32,1,2176]{2,1,0:T(1,128)S(1)} %bitcast.8), channel_id=1, replica_groups=mesh['far'=2,'near'=2,'line'=2,'chip'=2,'core'=2] {'core','near','line',..., dimensions={0} | all-to-all | bytes 557056 | tf_op jit(solution)/shard_map/all_to_all | solution.py:279
  28.8 0.1 shard_map.72.gain_ref
  28.9 0.3 %collective-permute-start.2 = (f32[8,256]{1,0:T(8,128)S(1)}, f32[8,256]{1,0:T(8,128)S(1)}, u32[]{:S(2)}, u32[]{:S(2)}) collective-permute-start(f32[8,256]{1,0:T(8,128)S(1)} %shard_map.72.gain_ref), channel_id=1, source_target_pairs={{0,1},{1,0},{2,3},{3,2},{4,5},{5,4},{6,7},{7,6},{8,9},{9,8},{10,11... | collective-permute-start | bytes 24584 | tf_op jit(solution)/shard_map/ppermute | solution.py:286
  29.2 0.9 %collective-permute-done.2.theirs_ref = f32[8,256]{1,0:T(8,128)S(1)} collective-permute-done((f32[8,256]{1,0:T(8,128)S(1)}, f32[8,256]{1,0:T(8,128)S(1)}, u32[]{:S(2)}, u32[]{:S(2)}) %collective-permute-start.2) | collective-permute-done | bytes 8224 | tf_op jit(solution)/shard_map/ppermute | solution.py:286
  30.1 0.7 %shard_map.73 = (f32[16,32]{1,0:T(8,128)}, f32[1,16]{1,0:T(1,128)}) custom-call(f32[8,256]{1,0:T(8,128)S(1)} %shard_map.72.gain_ref, f32[8,256]{1,0:T(8,128)S(1)} %collective-permute-done.2.theirs_ref), custom_call_target="tpu_custom_call" | custom-call | bytes 18496 | tf_op jit(solution)/shard_map/pallas_call | solution.py:38
Async XLA Ops:
  0.6 10.5 %collective-permute-start = (s32[2048,256]{1,0:T(8,128)}, s32[2048,256]{1,0:T(8,128)S(1)}, u32[]{:S(2)}, u32[]{:S(2)}) collective-permute-start(s32[2048,256]{1,0:T(8,128)} %refs_0_.1), channel_id=1, source_target_pairs={{0,1},{1,0},{2,3},{3,2},{4,5},{5,4},{6,7},{7,6},{8,9},{9,8},{10,11... | collective-permute-start | bytes 6291464 | tf_op jit(solution)/shard_map/ppermute | solution.py:239
  2.6 14.2 %all-to-all-start = ((f32[32,1,512]{2,1,0:T(1,128)}), f32[32,1,512]{2,1,0:T(1,128)S(1)}, u32[]{:S(2)}, u32[]{:S(2)}) async-start(f32[32,1,512]{2,1,0:T(1,128)} %bitcast.3), calls=%async_computation | async-start | bytes 131072 | tf_op jit(solution)/shard_map/all_to_all | solution.py:257
  9.6 1.6 %collective-permute-start.1 = (f32[3,2048]{1,0:T(4,128)S(1)}, f32[3,2048]{1,0:T(4,128)S(1)}, u32[]{:S(2)}, u32[]{:S(2)}) collective-permute-start(f32[3,2048]{1,0:T(4,128)S(1)} %get-tuple-element.10.row_ref), channel_id=1, source_target_pairs={{0,1},{1,0},{2,3},{3,2},{4,5},{5,4},{6,7},{7,6},{8,9},{9,8},{10,11... | collective-permute-start | bytes 73736 | tf_op jit(solution)/shard_map/ppermute | solution.py:260
  28.9 1.2 %collective-permute-start.2 = (f32[8,256]{1,0:T(8,128)S(1)}, f32[8,256]{1,0:T(8,128)S(1)}, u32[]{:S(2)}, u32[]{:S(2)}) collective-permute-start(f32[8,256]{1,0:T(8,128)S(1)} %shard_map.72.gain_ref), channel_id=1, source_target_pairs={{0,1},{1,0},{2,3},{3,2},{4,5},{5,4},{6,7},{7,6},{8,9},{9,8},{10,11... | collective-permute-start | bytes 24584 | tf_op jit(solution)/shard_map/ppermute | solution.py:286
